TPU v7x, 32 devices: a whole 2x2x4 slice. The times are simulated.
32 devices in a mesh: gx: 8 (over z, y), gy: 4 (over x, core).
Axes of the slice: x: 2, y: 2, z: 4, core: 2. Of those that a mesh axis runs over, the one named last changes fastest.
Arguments:
- features: bfloat16 [64, 8, 8, 8, 256], P(('gx', 'gy')), may hold values from -6 to 6
- cotangent: bfloat16 [64, 8, 8, 8, 256], P(('gx', 'gy')), may hold values from -6 to 6
- kernel: bfloat16 [27, 256, 256], replicated, may hold values from -0.078125 to 0.078125
- occupancy: int32 [64, 512], P(('gx', 'gy')), may hold values 0 or 1
- neighbors: int32 [64, 27], P(('gx', 'gy')), may hold values from -1 to 1, as said below
Outputs:
- out_features: bfloat16 [64, 8, 8, 8, 256], P(('gx', 'gy'))
- in_grad: bfloat16 [64, 8, 8, 8, 256], P(('gx', 'gy'))
- kernel_grad: float32 [27, 256, 256], replicated
Inputs may be any that keep to these rules, and one draw needn't show every extreme that they name: neighbors[b, k] is the slot of the occupied brick at level L + oz in column (cx + ox, cy + oy), where L is brick b's level, and -1 where that column lies outside the 8 x 4 grid or that brick is not occupied; each column holds 2 occupied bricks among 4 levels, slots in rising level; the offset k = 13 entry of a brick is its own slot.
All inputs are finite; a program needn't handle non-finite values. No bound on the sum of `occupancy` on one device may be relied on, other than what follows from the above.
Results may differ from a plain program's by a relative error of at most 0.001.
Values may be sent and summed in bfloat16 or wider, within the bound.
A program may use at most 128 MiB of HBM per device.

v0:
```python
import jax
import jax.numpy as jnp
from jax import lax
from jax.sharding import PartitionSpec as P

layer_pick = {-1: slice(7, 8), 0: slice(0, 8), 1: slice(0, 1)}


def extended(cells, sides, width):
    for axis, dim in sides:
        count = lax.axis_size(axis)
        ends = count - 1
        head = lax.slice_in_dim(cells, 0, width, axis=dim)
        tail = lax.slice_in_dim(cells, cells.shape[dim] - width, cells.shape[dim], axis=dim)
        cells = jnp.concatenate(
            [
                lax.ppermute(tail, axis, [(i, (i + 1) % count) for i in range(ends)]),
                cells,
                lax.ppermute(head, axis, [((i + 1) % count, i) for i in range(ends)]),
            ],
            axis=dim,
        )
    return cells


def assemble(source_of, neighbors, slots):
    chosen = jnp.where(neighbors >= 0, neighbors, slots)
    x_parts = []
    for ox in (-1, 0, 1):
        y_parts = []
        for oy in (-1, 0, 1):
            source = source_of(ox, oy)
            source = jnp.concatenate([source, jnp.zeros_like(source[:, :1])], 1)
            z_parts = []
            for oz in (-1, 0, 1):
                offset = 9 * (ox + 1) + 3 * (oy + 1) + (oz + 1)
                picked = jnp.take(source, chosen[:, offset], axis=1)
                z_parts.append(picked[:, :, :, :, layer_pick[oz]])
            y_parts.append(jnp.concatenate(z_parts, 4))
        x_parts.append(jnp.concatenate(y_parts, 3))
    return jnp.concatenate(x_parts, 2)


def combine_terms(terms, scale):
    return lax.psum(terms, ("gx", "gy")) * scale


def shards(features, cotangent, kernel, occupancy, neighbors):
    slots = features.shape[0]
    width = features.shape[-1]
    mask_b = occupancy.reshape(slots, 8, 8, 8, 1).astype(jnp.bfloat16)
    mask_f = occupancy.reshape(slots * 512, 1).astype(jnp.float32)
    masked = features * mask_b
    masked_grad = cotangent * mask_b
    both = jnp.stack([masked, masked_grad])
    beside_all = extended(both[None, None], (("gx", 0), ("gy", 1)), 1)

    def source_of(ox, oy):
        return beside_all[ox + 1, oy + 1][:, :, layer_pick[ox], layer_pick[oy]]

    padded = assemble(source_of, neighbors, slots)
    padded_in = padded[0]
    padded_grad = padded[1]
    flat_grad = masked_grad.reshape(-1, width)
    scale = jnp.float32(1.0 / (512.0 * slots * lax.axis_size("gx") * lax.axis_size("gy")) ** 0.5)
    forward = jnp.zeros((slots * 512, width), jnp.float32)
    terms = []
    for step_x in range(3):
        for step_y in range(3):
            for step_z in range(3):
                offset = 9 * step_x + 3 * step_y + step_z
                window = padded_in[
                    :, step_x : step_x + 8, step_y : step_y + 8, step_z : step_z + 8
                ].reshape(-1, width)
                forward = forward + jnp.dot(
                    window, kernel[offset], preferred_element_type=jnp.float32
                )
                terms.append(
                    lax.dot_general(
                        window,
                        flat_grad,
                        (((0,), (0,)), ((), ())),
                        preferred_element_type=jnp.float32,
                    )
                )
    forward, terms = (forward, jnp.stack(terms))
    backward = jnp.zeros((slots * 512, width), jnp.float32)
    for step_x in range(3):
        for step_y in range(3):
            for step_z in range(3):
                offset = 9 * step_x + 3 * step_y + step_z
                back_window = padded_grad[
                    :, 2 - step_x : 10 - step_x, 2 - step_y : 10 - step_y, 2 - step_z : 10 - step_z
                ].reshape(-1, width)
                backward = backward + lax.dot_general(
                    back_window,
                    kernel[offset],
                    (((1,), (1,)), ((), ())),
                    preferred_element_type=jnp.float32,
                )
    kernel_grad = combine_terms(terms, scale)
    out_features = (forward * mask_f).astype(jnp.bfloat16).reshape(slots, 8, 8, 8, width)
    in_grad = (backward * mask_f).astype(jnp.bfloat16).reshape(slots, 8, 8, 8, width)
    return (out_features, in_grad, kernel_grad)


def solution(mesh):
    placed = (
        P(("gx", "gy"), None, None, None, None),
        P(("gx", "gy"), None, None, None, None),
        P(),
        P(("gx", "gy"), None),
        P(("gx", "gy"), None),
    )
    return jax.shard_map(
        shards,
        mesh=mesh,
        in_specs=placed,
        out_specs=(
            P(("gx", "gy"), None, None, None, None),
            P(("gx", "gy"), None, None, None, None),
            P(),
        ),
        check_vma=False,
    )
```

profile of v0, /device:TPU:1, one launch (start us, length us, event | category | flops | bytes accessed | tf_op | source)
XLA Modules:
  0.0 374.2 jit_solution(3132860403979781320)
XLA Ops:
  8.1 1.4 fusion.34
  11.5 1.3 collective-permute-start.1
  12.8 5.6 %collective-permute-start = (bf16[1,1,2,2,8,8,8,256]{7,6,3,2,5,4,1,0:T(8,128)(2,1)}, bf16[1,1,2,2,8,8,8,256]{7,6,3,2,5,4,1,0:T(8,128)(2,1)}, u32[]{:S(2)}, u32[]{:S(2)}) collective-permute-start(bf16[1,1,2,2,8,8,8,256]{7,6,3,2,5,4,1,0:T(8,128)(2,1)} %get-tuple-element.97), channel_id=1, source_target_pairs={{0,4},{4,8},{8,12},{12,16},{16,20},{20,24},{24,28},{1,5},{5,9},{9,... | collective-permute-start | bytes 3145736 | tf_op jit(solution)/shard_map/ppermute | solution.py:17
  26.7 1.6 gather_fusion.14
  33.0 1.4 fusion.31
  34.4 4.2 %collective-permute-done.1 = bf16[1,1,2,2,8,8,8,256]{7,6,3,2,5,4,1,0:T(8,128)(2,1)} collective-permute-done((bf16[1,1,2,2,8,8,8,256]{7,6,3,2,5,4,1,0:T(8,128)(2,1)}, bf16[1,1,2,2,8,8,8,256]{7,6,3,2,5,4,1,0:T(8,128)(2,1)}, u32[]{:S(2)}, u32[]{:S(2)}) %collective-permute-start.1) | collective-permute-done | bytes 1048608 | tf_op jit(solution)/shard_map/ppermute | solution.py:19
  38.6 23.4 %collective-permute-done = bf16[1,1,2,2,8,8,8,256]{7,6,3,2,5,4,1,0:T(8,128)(2,1)} collective-permute-done((bf16[1,1,2,2,8,8,8,256]{7,6,3,2,5,4,1,0:T(8,128)(2,1)}, bf16[1,1,2,2,8,8,8,256]{7,6,3,2,5,4,1,0:T(8,128)(2,1)}, u32[]{:S(2)}, u32[]{:S(2)}) %collective-permute-start) | collective-permute-done | bytes 1048608 | tf_op jit(solution)/shard_map/ppermute | solution.py:17
  62.0 3.9 %pad_maximum_fusion = bf16[3,1,2,2,8,8,8,256]{7,6,3,2,5,4,1,0:T(8,128)(2,1)} fusion(bf16[1,1,2,2,8,8,8,256]{7,6,3,2,5,4,1,0:T(8,128)(2,1)} %collective-permute-done.1, bf16[1,1,2,2,8,8,8,256]{7,6,3,2,5,4,1,0:T(8,128)(2,1)} %get-tuple-element.97, bf16[1,1,2,2,8,8,8,256]{7,6,3,2,5,4,1,0:T(8,128)(2,1)} %collective-permute-done), kind=kLoop, calls=%fused_computation.29 | loop fusion | flops 3145728 | bytes 6291456 | tf_op jit(solution)/shard_map/concatenate | solution.py:15
  65.9 2.4 collective-permute-start.3
  68.9 1.1 fusion.33
  70.0 3.2 collective-permute-start.2
  74.5 2.2 slice.664
  88.2 16.5 %collective-permute-done.3 = bf16[3,1,2,2,8,8,8,256]{7,6,3,2,5,4,1,0:T(8,128)(2,1)} collective-permute-done((bf16[3,1,2,2,8,8,8,256]{7,6,3,2,5,4,1,0:T(8,128)(2,1)}, bf16[3,1,2,2,8,8,8,256]{7,6,3,2,5,4,1,0:T(8,128)(2,1)}, u32[]{:S(2)}, u32[]{:S(2)}) %collective-permute-start.3) | collective-permute-done | bytes 3145760 | tf_op jit(solution)/shard_map/ppermute | solution.py:19
  104.8 3.3 slice_bitcast_fusion.6
  110.9 3.2 slice_bitcast_fusion.7
  114.7 2.0 gather_fusion.20
  116.7 1.3 copy.211
  118.0 2.0 gather_fusion.19
  120.0 2.0 gather_fusion.18
  122.0 1.3 copy.212
  148.0 2.7 maximum_maximum_fusion
  151.0 2.5 fusion.203
  153.5 4.4 %fusion.202 = (bf16[2,8,8,8,256]{4,3,2,1,0:T(8,128)(2,1)}, bf16[2,8,8,8,256]{4,3,2,1,0:T(8,128)(2,1)}, bf16[2,8,8,8,256]{4,3,2,1,0:T(8,128)(2,1)}, bf16[2,8,8,8,...) fusion(bf16[2,10,10,10,256]{4,3,2,1,0:T(8,128)(2,1)S(1)} %get-t, ...), kind=kLoop, calls=%fused_computation.483 | loop fusion | bytes 19922944 | tf_op jit(solution)/shard_map/slice | solution.py:72
  157.9 2.3 fusion.201
  160.2 4.2 %fusion.200 = (bf16[2,8,8,8,256]{4,3,2,1,0:T(8,128)(2,1)}, bf16[2,8,8,8,256]{4,3,2,1,0:T(8,128)(2,1)}, bf16[2,8,8,8,256]{4,3,2,1,0:T(8,128)(2,1)}, bf16[2,8,8,8,...) fusion(bf16[2,10,10,10,256]{4,3,2,1,0:T(8,128)(2,1)S(1)} %get-t, ...), kind=kLoop, calls=%fused_computation.481 | loop fusion | bytes 19922944 | tf_op jit(solution)/shard_map/slice | solution.py:92
  166.5 1.3 fusion.89
  167.7 1.3 fusion.87
  196.7 1.8 convolution_add_fusion.51
  198.5 1.4 convolution_add_fusion.50
  219.6 1.1 fusion.3
  220.7 139.7 %all-reduce.11.cloned.1.call-done = f32[27,256,256]{2,1,0:T(8,128)} async-done(((f32[27,256,256]{2,1,0:T(8,128)}), f32[27,256,256]{2,1,0:T(8,128)}) %all-reduce.11.cloned.1.call-update) | async-done | bytes 7077904 | tf_op jit(solution)/shard_map/psum | solution.py:45
  360.4 6.9 %broadcast_multiply_fusion = f32[27,256,256]{2,1,0:T(8,128)} fusion(f32[27,256,256]{2,1,0:T(8,128)} %all-reduce.11.cloned.1.call-done), kind=kLoop, calls=%fused_computation.27 | loop fusion | flops 1769472 | bytes 14155776 | tf_op jit(solution)/shard_map/mul | solution.py:45
  (354 shorter events, 105.9 us)
Async XLA Ops:
  7.2 11.2 %copy-start.61 = (s32[2,27]{1,0:T(2,128)S(1)}, s32[2,27]{1,0:T(2,128)}, u32[]{:S(2)}) copy-start(s32[2,27]{1,0:T(2,128)} %param.17) | copy-start | bytes 652
  7.2 353.2 %all-reduce.11.cloned.1.call-start = ((), (), s32[]{:S(2)}) async-start(), calls=%async_computation | async-start | bytes 14155776 | tf_op jit(solution)/shard_map/psum | solution.py:45
  11.5 27.2 %collective-permute-start.1 = (bf16[1,1,2,2,8,8,8,256]{7,6,3,2,5,4,1,0:T(8,128)(2,1)}, bf16[1,1,2,2,8,8,8,256]{7,6,3,2,5,4,1,0:T(8,128)(2,1)}, u32[]{:S(2)}, u32[]{:S(2)}) collective-permute-start(bf16[1,1,2,2,8,8,8,256]{7,6,3,2,5,4,1,0:T(8,128)(2,1)} %get-tuple-element.97), channel_id=1, source_target_pairs={{4,0},{8,4},{12,8},{16,12},{20,16},{24,20},{28,24},{5,1},{9,5},{13... | collective-permute-start | bytes 3145736 | tf_op jit(solution)/shard_map/ppermute | solution.py:19
  12.8 49.2 %collective-permute-start = (bf16[1,1,2,2,8,8,8,256]{7,6,3,2,5,4,1,0:T(8,128)(2,1)}, bf16[1,1,2,2,8,8,8,256]{7,6,3,2,5,4,1,0:T(8,128)(2,1)}, u32[]{:S(2)}, u32[]{:S(2)}) collective-permute-start(bf16[1,1,2,2,8,8,8,256]{7,6,3,2,5,4,1,0:T(8,128)(2,1)} %get-tuple-element.97), channel_id=1, source_target_pairs={{0,4},{4,8},{8,12},{12,16},{16,20},{20,24},{24,28},{1,5},{5,9},{9,... | collective-permute-start | bytes 3145736 | tf_op jit(solution)/shard_map/ppermute | solution.py:17
  65.9 38.9 %collective-permute-start.3 = (bf16[3,1,2,2,8,8,8,256]{7,6,3,2,5,4,1,0:T(8,128)(2,1)}, bf16[3,1,2,2,8,8,8,256]{7,6,3,2,5,4,1,0:T(8,128)(2,1)}, u32[]{:S(2)}, u32[]{:S(2)}) collective-permute-start(bf16[3,1,2,2,8,8,8,256]{7,6,3,2,5,4,1,0:T(8,128)(2,1)} %pad_maximum_fusion), channel_id=1, source_target_pairs={{1,0},{2,1},{3,2},{5,4},{6,5},{7,6},{9,8},{10,9},{11,10},{13,12},{... | collective-permute-start | bytes 9437192 | tf_op jit(solution)/shard_map/ppermute | solution.py:19
  70.0 40.9 %collective-permute-start.2 = (bf16[3,1,2,2,8,8,8,256]{7,6,3,2,5,4,1,0:T(8,128)(2,1)}, bf16[3,1,2,2,8,8,8,256]{7,6,3,2,5,4,1,0:T(8,128)(2,1)}, u32[]{:S(2)}, u32[]{:S(2)}) collective-permute-start(bf16[3,1,2,2,8,8,8,256]{7,6,3,2,5,4,1,0:T(8,128)(2,1)} %pad_maximum_fusion), channel_id=1, source_target_pairs={{0,1},{1,2},{2,3},{4,5},{5,6},{6,7},{8,9},{9,10},{10,11},{12,13},{... | collective-permute-start | bytes 9437192 | tf_op jit(solution)/shard_map/ppermute | solution.py:17
  123.4 24.6 %copy-start.54 = (bf16[2,2,8,8,1,256]{5,4,3,2,1,0:T(2,128)(2,1)S(1)}, bf16[2,2,8,8,1,256]{5,4,3,2,1,0:T(2,128)(2,1)}, u32[]{:S(2)}) copy-start(bf16[2,2,8,8,1,256]{5,4,3,2,1,0:T(2,128)(2,1)} %slice.664) | copy-start | bytes 393220
  123.4 24.6 %copy-start.55 = (bf16[2,2,1,8,8,256]{5,4,3,2,1,0:T(8,128)(2,1)S(1)}, bf16[2,2,1,8,8,256]{5,4,3,2,1,0:T(8,128)(2,1)}, u32[]{:S(2)}) copy-start(bf16[2,2,1,8,8,256]{5,4,3,2,1,0:T(8,128)(2,1)} %bitcast_select_fusion.3) | copy-start | bytes 393220
  127.0 20.9 %copy-start.62 = (pred[2]{0:T(512)(128)(4,1)S(1)}, pred[2]{0:T(512)(128)(4,1)}, u32[]{:S(2)}) copy-start(pred[2]{0:T(512)(128)(4,1)} %compare_and_fusion.26) | copy-start | bytes 10
  127.0 21.0 %copy-start.56 = (bf16[2,2,1,8,1,256]{5,4,3,2,1,0:T(2,128)(2,1)S(1)}, bf16[2,2,1,8,1,256]{5,4,3,2,1,0:T(2,128)(2,1)}, u32[]{:S(2)}) copy-start(bf16[2,2,1,8,1,256]{5,4,3,2,1,0:T(2,128)(2,1)} %broadcast_select_fusion) | copy-start | bytes 49156
  127.0 21.0 %copy-start.57 = (bf16[2,2,1,8,1,256]{5,4,3,2,1,0:T(2,128)(2,1)S(1)}, bf16[2,2,1,8,1,256]{5,4,3,2,1,0:T(2,128)(2,1)}, u32[]{:S(2)}) copy-start(bf16[2,2,1,8,1,256]{5,4,3,2,1,0:T(2,128)(2,1)} %broadcast_select_fusion.1) | copy-start | bytes 49156
  127.0 21.0 %copy-start.58 = (bf16[2,2,1,8,1,256]{5,4,3,2,1,0:T(2,128)(2,1)S(1)}, bf16[2,2,1,8,1,256]{5,4,3,2,1,0:T(2,128)(2,1)}, u32[]{:S(2)}) copy-start(bf16[2,2,1,8,1,256]{5,4,3,2,1,0:T(2,128)(2,1)} %broadcast_select_fusion.6) | copy-start | bytes 49156
  127.0 21.0 %copy-start.59 = (bf16[2,2,1,8,1,256]{5,4,3,2,1,0:T(2,128)(2,1)S(1)}, bf16[2,2,1,8,1,256]{5,4,3,2,1,0:T(2,128)(2,1)}, u32[]{:S(2)}) copy-start(bf16[2,2,1,8,1,256]{5,4,3,2,1,0:T(2,128)(2,1)} %broadcast_select_fusion.7) | copy-start | bytes 49156
  160.2 4.2 %copy-start.53 = (bf16[2,8,8,8,256]{4,3,0,2,1:T(8,128)(2,1)S(1)}, bf16[2,8,8,8,256]{4,3,0,2,1:T(8,128)(2,1)}, u32[]{:S(2)}) copy-start(bf16[2,8,8,8,256]{4,3,0,2,1:T(8,128)(2,1)} %copy-done.52) | copy-start | bytes 1572868
  164.4 2.1 copy-start
  196.7 3.2 copy-start.51
  196.7 3.5 copy-start.50
  198.5 2.0 copy-start.49
  201.6 1.3 copy-start.43
  202.0 1.3 copy-start.42
  202.4 1.3 copy-start.41
  202.9 1.2 copy-start.40
  203.7 1.3 copy-start.38
  204.1 1.2 copy-start.37
  204.5 1.2 copy-start.36
  207.6 1.3 copy-start.1
  207.6 1.5 copy-start.30
  207.9 1.5 copy-start.28
  208.4 1.4 copy-start.26
  213.6 1.8 copy-start.14
  214.0 1.8 copy-start.13
  214.3 1.8 copy-start.12
  (36 other events, 40.2 us)
Sparse Core Ops, SparseCore 0:
  196.8 163.5 all-reduce.10
where the time goes:
time: 377 us; the launch traced here: 374 us
  waiting for transfers between devices  184 us (49%)
  local copies, waits for them, and re-layouts  60.1 us (16%)
  matrix products  51.9 us (14%)
  other arithmetic  50.5 us (13%)
  between operations  15.5 us (4%)
  starting transfers between devices  12.5 us (3%)
    psum x1, waiting for transfers between devices, combine_terms(): return lax.psum(terms, ('gx', 'gy')) * scale  140 us
    dot_general x27, matrix products, shards(): lax.dot_general(window, flat_grad, (((0,), (0,)), ((), ())), preferred_el...  28.6 us
    gather x43, local copies, waits for them, and re-layouts, assemble(): picked = jnp.take(source, chosen[:, offset], axis=1)  27.2 us
    ppermute x2, waiting for transfers between devices, extended(): lax.ppermute(tail, axis, [(i, (i + 1) % count) for i in range(ends)])  23.4 us
    ppermute x2, waiting for transfers between devices, extended(): lax.ppermute(head, axis, [((i + 1) % count, i) for i in range(ends)])  20.7 us
    select_n x45, other arithmetic, assemble(): picked = jnp.take(source, chosen[:, offset], axis=1)  19.6 us
    dot_general x27, matrix products, shards(): jnp.dot(window, kernel[offset], preferred_element_type=jnp.float32)  12.5 us
    dot_general x27, matrix products, shards(): lax.dot_general(back_window, kernel[offset], (((1,), (1,)), ((), ())), pr...  10.7 us
  transfers between devices with their start and end apart: 5, of which 4 were waited for; matrix products, arithmetic and copies ran while one was open for 16% of the time, Pallas kernels for 0%

commit v1 on v0

v1 whole, which is shorter than its diff:
```python
import functools

import jax
import jax.numpy as jnp
from jax import lax
from jax.experimental import pallas as pl
from jax.experimental.pallas import tpu as pltpu
from jax.sharding import PartitionSpec as P

MESH = pl.DeviceIdType.MESH
VMEM = pltpu.VMEM
PARTS = 3
LANES = 128


def shift_by_one(cells, axis):
    count = lax.axis_size(axis)
    ends = count - 1
    head = lambda dim: lax.slice_in_dim(cells, 0, 1, axis=dim)
    tail = lambda dim: lax.slice_in_dim(cells, cells.shape[dim] - 1, cells.shape[dim], axis=dim)
    up = [(i, i + 1) for i in range(ends)]
    down = [(i + 1, i) for i in range(ends)]
    return lambda dim: jnp.concatenate(
        [lax.ppermute(tail(dim), axis, up), cells, lax.ppermute(head(dim), axis, down)], axis=dim
    )


def spread(table, dim):
    first = lax.slice_in_dim(table, 0, 1, axis=dim)
    middle = lax.slice_in_dim(table, 1, 2, axis=dim)
    last = lax.slice_in_dim(table, 2, 3, axis=dim)
    return jnp.concatenate([first] + [middle] * 8 + [last], axis=dim)


def z_shifted(both, neighbors):
    slots = both.shape[1]
    wide = shift_by_one(both, "gx")(2)
    wide = shift_by_one(wide, "gy")(3)
    table = spread(spread(neighbors.reshape(slots, 3, 3, 3), 1), 2)

    def pick(layer, oz):
        total = None
        for slot in range(slots):
            hit = (table[:, :, :, oz] == slot)[None, :, :, :, None, None]
            part = jnp.where(hit, wide[:, slot : slot + 1, :, :, layer], jnp.zeros((), wide.dtype))
            total = part if total is None else total + part
        return total

    low = pick(slice(7, 8), 0)
    mid = pick(slice(0, 8), 1)
    high = pick(slice(0, 1), 2)
    return jnp.stack(
        [
            jnp.concatenate([low, mid[..., :7, :]], 4),
            mid,
            jnp.concatenate([mid[..., 1:, :], high], 4),
        ]
    )


def conv_kernel(slots, even_ref, odd_ref, w_ref, wt_ref, grad_t_ref, mask_ref, out_ref, back_ref, terms_ref, acc_f, acc_b):
    ox = pl.program_id(0)

    def window(tensor, brick, oy, oz):
        if oy == 1:
            value = odd_ref[oz, tensor, brick, pl.ds(ox, 8)]
        else:
            value = even_ref[oz, tensor, brick, pl.ds(ox, 8), 8 * oy : 8 * oy + 64]
        return value.reshape(512, value.shape[-1])

    for oy in range(3):
        weights = w_ref[3 * oy : 3 * oy + 3].reshape(-1, w_ref.shape[-1])
        weights_t = wt_ref[3 * oy : 3 * oy + 3].reshape(-1, wt_ref.shape[-1])
        for brick in range(slots):
            rows = slice(512 * brick, 512 * brick + 512)
            for tensor, acc, rhs in ((0, acc_f, weights), (1, acc_b, weights_t)):
                lhs = jnp.concatenate([window(tensor, brick, oy, oz) for oz in range(3)], 1)
                part = jnp.dot(lhs, rhs, preferred_element_type=jnp.float32)
                if oy == 0:
                    @pl.when(ox == 0)
                    def _():
                        acc[rows] = part

                    @pl.when(ox != 0)
                    def _():
                        acc[rows] += part
                else:
                    acc[rows] += part
        for oz in range(3):
            both = jnp.concatenate([window(0, brick, oy, oz) for brick in range(slots)], 0)
            term = jnp.dot(grad_t_ref[...], both, preferred_element_type=jnp.float32)
            terms_ref[3 * oy + oz] = term.T

    @pl.when(ox == 2)
    def _():
        out_ref[...] = (acc_f[...] * mask_ref[...]).astype(out_ref.dtype)
        back_ref[...] = (acc_b[...] * mask_ref[...]).astype(back_ref.dtype)


def conv(even, odd, weights, weights_t, grad_t, mask):
    slots = even.shape[2]
    width = even.shape[-1]
    rows = slots * 512
    whole = lambda array: pl.BlockSpec(array.shape, lambda i: (0,) * array.ndim)
    nine = pl.BlockSpec((9, width, width), lambda i: (i, 0, 0))
    flat = pl.BlockSpec((rows, width), lambda i: (0, 0))
    return pl.pallas_call(
        functools.partial(conv_kernel, slots),
        grid=(3,),
        in_specs=[whole(even), whole(odd), nine, nine, whole(grad_t), whole(mask)],
        out_specs=[flat, flat, nine],
        out_shape=[
            jax.ShapeDtypeStruct((rows, width), jnp.bfloat16),
            jax.ShapeDtypeStruct((rows, width), jnp.bfloat16),
            jax.ShapeDtypeStruct((27, width, width), jnp.float32),
        ],
        scratch_shapes=[VMEM((rows, width), jnp.float32), VMEM((rows, width), jnp.float32)],
        compiler_params=pltpu.CompilerParams(
            dimension_semantics=("arbitrary",), vmem_limit_bytes=56 * 2**20
        ),
        cost_estimate=pl.CostEstimate(
            flops=27 * 6 * rows * width * width, bytes_accessed=24 * 2**20, transcendentals=0
        ),
    )(even, odd, weights, weights_t, grad_t, mask)


def reduce_kernel(pair, orders, scale, terms_ref, out_ref, acc, *rest):
    stages = len(orders[0]) + 1
    recv, (send_sem, recv_sem) = rest[:stages], rest[stages:]
    part_rows = acc.shape[1]
    place = {"gx": lax.axis_index("gx"), "gy": lax.axis_index("gy")}

    def bit_of(bit):
        axis, step = bit
        return (place[axis] // step) % 2

    def partner(bit):
        axis, step = bit
        there = dict(place)
        there[axis] = place[axis] + step - 2 * step * bit_of(bit)
        return (there["gx"], there["gy"])

    barrier = pltpu.get_barrier_semaphore()
    for bit in [pair] + sorted(orders[0]):
        pl.semaphore_signal(barrier, inc=1, device_id=partner(bit), device_id_type=MESH)
    pl.semaphore_wait(barrier, stages)

    side = bit_of(pair)
    mine = pl.ds(pl.multiple_of(side * LANES, LANES), LANES)
    other = pl.ds(pl.multiple_of((1 - side) * LANES, LANES), LANES)
    started = []

    def send(src, dst, step, part, bit):
        copy = pltpu.make_async_remote_copy(
            src_ref=src,
            dst_ref=dst,
            send_sem=send_sem.at[step, part],
            recv_sem=recv_sem.at[step, part],
            device_id=partner(bit),
            device_id_type=MESH,
        )
        copy.start()
        started.append(copy)
        return copy

    base = [0] * PARTS
    flying = [
        send(terms_ref.at[pl.ds(p * part_rows, part_rows), other], recv[0].at[p], 0, p, pair)
        for p in range(PARTS)
    ]
    for stage in range(stages):
        size = part_rows >> stage
        half = size // 2
        block = min(size, 144)
        for p in range(PARTS):
            flying[p].wait_recv()

            @pl.loop(0, size // block)
            def _(i):
                here = pl.ds(pl.multiple_of(i * block, 16), block)
                there = pl.ds(pl.multiple_of(base[p] + i * block, 16), block)
                if stage == 0:
                    there_in = pl.ds(pl.multiple_of(p * part_rows + i * block, 16), block)
                    acc[p, here] = terms_ref[there_in, mine] + recv[0][p, here]
                else:
                    acc[p, there] = acc[p, there] + recv[stage][p, here]

            if stage < stages - 1:
                bit = orders[p][stage]
                away = pl.multiple_of(base[p] + (1 - bit_of(bit)) * half, 16)
                base[p] = base[p] + bit_of(bit) * half
                flying[p] = send(acc.at[p, pl.ds(away, half)], recv[stage + 1].at[p], stage + 1, p, bit)
            else:
                own = pl.ds(pl.multiple_of(base[p], 16), size)
                full = pl.ds(pl.multiple_of(p * part_rows + base[p], 16), size)
                out_ref[full, mine] = acc[p, own] * scale
                span = out_ref.at[full, mine]
                flying[p] = send(span, span, stages, p, orders[p][-1])
    for back in range(1, stages + 1):
        level = stages - 1 - back
        size = part_rows >> level if level >= 0 else 0
        for p in range(PARTS):
            flying[p].wait_recv()
            if level < 0:
                continue
            base[p] = base[p] - bit_of(orders[p][level]) * (size // 2)
            full = pl.ds(pl.multiple_of(p * part_rows + base[p], 16), size)
            span = out_ref.at[full, mine]
            flying[p] = send(span, span, stages + back, p, orders[p][level - 1] if level > 0 else pair)
    for copy in started:
        copy.wait_send()


def sum_plan(mesh, rows):
    sizes = dict(mesh.shape)
    if sizes["gx"] != 8 or sizes["gy"] != 4 or rows % (PARTS * 16 * 16):
        return None
    pair, x, y, z_near, z_far = ("gy", 1), ("gy", 2), ("gx", 1), ("gx", 2), ("gx", 4)
    return pair, [[x, y, z_near, z_far], [y, x, z_near, z_far], [z_near, z_far, x, y]]


def sum_devices(plan, terms, scale):
    width = terms.shape[-1]
    if plan is None or width != 2 * LANES:
        return lax.psum(terms, ("gx", "gy")) * jnp.float32(scale)
    pair, orders = plan
    flat = terms.reshape(-1, width)
    part_rows = flat.shape[0] // PARTS
    stages = len(orders[0]) + 1
    steps = 2 * stages
    out = pl.pallas_call(
        functools.partial(reduce_kernel, pair, orders, scale),
        in_specs=[pl.BlockSpec(memory_space=VMEM)],
        out_specs=pl.BlockSpec(memory_space=VMEM),
        out_shape=jax.ShapeDtypeStruct(flat.shape, jnp.float32),
        scratch_shapes=[VMEM((PARTS, part_rows, LANES), jnp.float32)]
        + [VMEM((PARTS, part_rows >> s, LANES), jnp.float32) for s in range(stages)]
        + [pltpu.SemaphoreType.DMA((steps, PARTS)), pltpu.SemaphoreType.DMA((steps, PARTS))],
        compiler_params=pltpu.CompilerParams(
            collective_id=0, has_side_effects=True, vmem_limit_bytes=48 * 2**20
        ),
    )(flat)
    return out.reshape(terms.shape)


def shards(plan, features, cotangent, kernel, occupancy, neighbors):
    slots = features.shape[0]
    width = features.shape[-1]
    mask_b = occupancy.reshape(slots, 8, 8, 8, 1).astype(jnp.bfloat16)
    mask_f = occupancy.reshape(slots * 512, 1).astype(jnp.float32)
    masked = features * mask_b
    masked_grad = cotangent * mask_b
    both = jnp.stack([masked, masked_grad])
    shifted = z_shifted(both, neighbors)
    even = shifted.reshape(3, 2, slots, 10, 80, width)
    odd = shifted[:, :, :, :, 1:9].reshape(3, 2, slots, 10, 64, width)
    flipped = jnp.flip(kernel, 0).transpose(0, 2, 1)
    grad_t = masked_grad.reshape(-1, width).T
    out, back, terms = conv(even, odd, kernel, flipped, grad_t, mask_f)
    scale = 1.0 / (512.0 * slots * lax.axis_size("gx") * lax.axis_size("gy")) ** 0.5
    kernel_grad = sum_devices(plan, terms, scale)
    return out.reshape(features.shape), back.reshape(features.shape), kernel_grad


def solution(mesh):
    placed = (
        P(("gx", "gy"), None, None, None, None),
        P(("gx", "gy"), None, None, None, None),
        P(),
        P(("gx", "gy"), None),
        P(("gx", "gy"), None),
    )
    plan = sum_plan(mesh, 27 * 256)
    return jax.shard_map(
        functools.partial(shards, plan),
        mesh=mesh,
        in_specs=placed,
        out_specs=(
            P(("gx", "gy"), None, None, None, None),
            P(("gx", "gy"), None, None, None, None),
            P(),
        ),
        check_vma=False,
    )
```

time: 377 us -> 171 us (0.45)
  the two profiles are of different devices: /device:TPU:1 before, /device:TPU:21 now
where the time goes in v1:
time: 171 us
  Pallas kernels  122 us (71%)
  local copies, waits for them, and re-layouts  20.8 us (12%)
  other arithmetic  15.5 us (9%)
  starting transfers between devices  11.6 us (7%)
    pallas_call x1, Pallas kernels, sum_devices(): pl.pallas_call(functools.partial(reduce_kernel, pair, orders, scale), in_...  98.4 us
    pallas_call x1, Pallas kernels, conv(): pl.pallas_call(functools.partial(conv_kernel, slots), grid=(3,), in_specs...  23.1 us
    unnamed x13, local copies, waits for them, and re-layouts  13.6 us
    ppermute x2, starting transfers between devices, shift_by_one(): lax.ppermute(tail(dim), axis, up)  7.39 us
    another operation x3, other arithmetic, z_shifted(): jnp.stack([jnp.concatenate([low, mid[..., :7, :]], 4), mid, jnp.concatena...  4.32 us
    ppermute x2, starting transfers between devices, shift_by_one(): lax.ppermute(head(dim), axis, down)  4.24 us
    transpose x1, local copies, waits for them, and re-layouts, shards(): flipped = jnp.flip(kernel, 0).transpose(0, 2, 1)  4.14 us
    add x4, other arithmetic, pick(): total = part if total is None else total + part  3.46 us
  transfers between devices with their start and end apart: 4, of which 1 were waited for; matrix products, arithmetic and copies ran while one was open for 9% of the time, Pallas kernels for 0%

profile of v1, /device:TPU:21, one launch (start us, length us, event | category | flops | bytes accessed | tf_op | source)
XLA Modules:
  0.0 170.8 jit_solution(5314940532322093454)
XLA Ops:
  0.6 0.8 convert_bitcast_fusion
  1.5 1.4 multiply_bitcast_fusion
  3.0 3.1 %collective-permute-start = (bf16[2,2,1,8,8,256]{5,4,3,2,1,0:T(8,128)(2,1)S(1)}, bf16[2,2,1,8,8,256]{5,4,3,2,1,0:T(8,128)(2,1)S(1)}, u32[]{:S(2)}, u32[]{:S(2)}) collective-permute-start(bf16[2,2,1,8,8,256]{5,4,3,2,1,0:T(8,128)(2,1)S(1)} %get-tuple-element.30), channel_id=1, source_target_pairs={{0,4},{4,8},{8,12},{12,16},{16,20},{20,24},{24,28},{1,5},{5,9},{9,... | collective-permute-start | bytes 393224 | tf_op jit(solution)/shard_map/ppermute | solution.py:24
  6.1 2.1 %collective-permute-start.1 = (bf16[2,2,1,8,8,256]{5,4,3,2,1,0:T(8,128)(2,1)S(1)}, bf16[2,2,1,8,8,256]{5,4,3,2,1,0:T(8,128)(2,1)S(1)}, u32[]{:S(2)}, u32[]{:S(2)}) collective-permute-start(bf16[2,2,1,8,8,256]{5,4,3,2,1,0:T(8,128)(2,1)S(1)} %get-tuple-element.31), channel_id=1, source_target_pairs={{4,0},{8,4},{12,8},{16,12},{20,16},{24,20},{28,24},{5,1},{9,5},{13... | collective-permute-start | bytes 393224 | tf_op jit(solution)/shard_map/ppermute | solution.py:24
  8.5 0.1 concatenate.22
  8.6 2.2 %compare_reduce_fusion.4 = (pred[2,10,10]{2,1,0:T(8,128)(4,1)S(1)}, pred[2,10,10]{2,1,0:T(8,128)(4,1)S(1)}, pred[2,10,10]{2,1,0:T(8,128)(4,1)S(1)}, pred[2,10,10...) fusion(s32[2,10,10,3]{3,2,1,0:T(8,128)S(1)} %concatenate.22), kind=kLoop, calls=%fused_computation.39 | loop fusion | flops 1200 | bytes 3600 | tf_op jit(solution)/shard_map/eq | solution.py:44
  10.9 0.1 copy.91
  11.0 0.1 copy.89
  11.4 1.1 copy.101
  12.4 1.0 copy.98
  13.5 5.7 %copy.97 = bf16[27,256,256]{1,2,0:T(8,128)(2,1)} copy(bf16[27,256,256]{2,1,0:T(8,128)(2,1)} %w_ref.1) | data formatting | bytes 7077888 | tf_op args[2]
  19.3 4.2 %collective-permute-start.2 = (bf16[2,2,10,1,8,256]{5,4,3,2,1,0:T(8,128)(2,1)S(1)}, bf16[2,2,10,1,8,256]{5,4,3,2,1,0:T(8,128)(2,1)S(1)}, u32[]{:S(2)}, u32[]{:S(2)}) collective-permute-start(bf16[2,2,10,1,8,256]{5,4,3,2,1,0:T(8,128)(2,1)S(1)} %get-tuple-element.28), channel_id=1, source_target_pairs={{0,1},{1,2},{2,3},{4,5},{5,6},{6,7},{8,9},{9,10},{10,11},{12,13},{... | collective-permute-start | bytes 491528 | tf_op jit(solution)/shard_map/ppermute | solution.py:24
  23.5 2.1 %collective-permute-start.3 = (bf16[2,2,10,1,8,256]{5,4,3,2,1,0:T(8,128)(2,1)S(1)}, bf16[2,2,10,1,8,256]{5,4,3,2,1,0:T(8,128)(2,1)S(1)}, u32[]{:S(2)}, u32[]{:S(2)}) collective-permute-start(bf16[2,2,10,1,8,256]{5,4,3,2,1,0:T(8,128)(2,1)S(1)} %get-tuple-element.29), channel_id=1, source_target_pairs={{1,0},{2,1},{3,2},{5,4},{6,5},{7,6},{9,8},{10,9},{11,10},{13,12},{... | collective-permute-start | bytes 491528 | tf_op jit(solution)/shard_map/ppermute | solution.py:24
  25.6 4.1 %reverse_bitcast_fusion.wt_ref = bf16[27,256,256]{2,1,0:T(8,128)(2,1)} fusion(bf16[27,256,256]{1,2,0:T(8,128)(2,1)} %copy.97), kind=kLoop, calls=%fused_computation.4 | loop fusion | bytes 7077888 | tf_op jit(solution)/shard_map/transpose | solution.py:257
  29.7 0.4 collective-permute-done.3
  30.1 0.3 pad_maximum_fusion.3
  30.5 0.2 slice_bitcast_fusion.2
  30.7 0.6 select_add_fusion
  31.4 0.6 select_add_fusion.2
  32.0 0.2 pad_maximum_fusion.8
  32.2 0.1 copy.108
  32.3 0.5 pad_maximum_fusion.9
  33.3 0.5 fusion.7
  33.8 1.6 fusion.5
  35.5 0.8 fusion.3
  36.3 0.8 fusion.1
  37.1 2.2 %fusion.odd_ref = bf16[3,2,2,10,64,256]{5,4,3,2,1,0:T(8,128)(2,1)} fusion(bf16[1,2,2,10,10,8,256]{6,5,4,3,2,1,0:T(8,128)(2,1)S(1)} %get-tuple-element.17, bf16[1,2,2,10,10,8,256]{6,5,4,3,2,1,0:T(8,128)(2,1)S(1)} %select_add_fusion, bf16[1,2,2,10,10,8,256]{6,5,4,3,2,1,0:T(8,128)(2,1)S(1)} %get-tuple-element.15), kind=kLoop, calls=%fused_computation.2 | loop fusion | flops 3932160 | bytes 8847360 | tf_op jit(solution)/shard_map/reshape | solution.py:256
  39.2 0.6 select_add_fusion.1
  39.8 2.7 %pad_maximum_fusion.even_ref = bf16[3,2,2,10,80,256]{5,4,3,2,1,0:T(8,128)(2,1)} fusion(bf16[1,2,2,10,80,256]{5,4,3,2,1,0:T(8,128)(2,1)S(1)} %get-tuple-element.18, bf16[1,2,2,10,80,256]{5,4,3,2,1,0:T(8,128)(2,1)S(1)} %select_add_fusion.1, bf16[1,2,2,10,80,256]{5,4,3,2,1,0:T(8,128)(2,1)S(1)} %get-tuple-element.16), kind=kLoop, calls=%fused_computation | loop fusion | flops 4915200 | bytes 9830400 | tf_op jit(solution)/shard_map/stack | solution.py:52
  42.6 23.1 %shard_map.76 = (bf16[1024,256]{1,0:T(8,128)(2,1)}, bf16[1024,256]{1,0:T(8,128)(2,1)}, f32[27,256,256]{2,1,0:T(8,128)}) custom-call(bf16[3,2,2,10,80,256]{5,4,3,2,1,0:T(8,128)(2,1)} %pad_maximum_fusion.even_ref, bf16[3,2,2,10,64,256]{5,4,3,2,1,0:T(8,128)(2,1)} %fusion.odd_ref, bf16[27,256,256]{2,1,0:T(8,128)(2,1)} %w_ref.1, ...), custom_call_target="tpu_custom_call" | custom-call | flops 10871635968 | bytes 25165824 | tf_op jit(solution)/shard_map/pallas_call | solution.py:107
  65.7 98.4 %shard_map.77 = f32[6912,256]{1,0:T(8,128)} custom-call(f32[6912,256]{1,0:T(8,128)} %bitcast.57), custom_call_target="tpu_custom_call" | custom-call | tf_op jit(solution)/shard_map/pallas_call | solution.py:231
  164.1 6.7 %copy.118 = f32[27,256,256]{2,1,0:T(8,128)} copy(f32[27,256,256]{2,1,0:T(8,128)} %bitcast.50) | data formatting | bytes 14155776
  (31 shorter events, 1.0 us)
Async XLA Ops:
  1.5 6.8 %copy-start = (s32[2,27]{1,0:T(2,128)S(1)}, s32[2,27]{1,0:T(2,128)}, u32[]{:S(2)}) copy-start(s32[2,27]{1,0:T(2,128)} %param.9) | copy-start | bytes 652
  3.0 16.2 %collective-permute-start = (bf16[2,2,1,8,8,256]{5,4,3,2,1,0:T(8,128)(2,1)S(1)}, bf16[2,2,1,8,8,256]{5,4,3,2,1,0:T(8,128)(2,1)S(1)}, u32[]{:S(2)}, u32[]{:S(2)}) collective-permute-start(bf16[2,2,1,8,8,256]{5,4,3,2,1,0:T(8,128)(2,1)S(1)} %get-tuple-element.30), channel_id=1, source_target_pairs={{0,4},{4,8},{8,12},{12,16},{16,20},{20,24},{24,28},{1,5},{5,9},{9,... | collective-permute-start | bytes 393224 | tf_op jit(solution)/shard_map/ppermute | solution.py:24
  6.1 13.1 %collective-permute-start.1 = (bf16[2,2,1,8,8,256]{5,4,3,2,1,0:T(8,128)(2,1)S(1)}, bf16[2,2,1,8,8,256]{5,4,3,2,1,0:T(8,128)(2,1)S(1)}, u32[]{:S(2)}, u32[]{:S(2)}) collective-permute-start(bf16[2,2,1,8,8,256]{5,4,3,2,1,0:T(8,128)(2,1)S(1)} %get-tuple-element.31), channel_id=1, source_target_pairs={{4,0},{8,4},{12,8},{16,12},{20,16},{24,20},{28,24},{5,1},{9,5},{13... | collective-permute-start | bytes 393224 | tf_op jit(solution)/shard_map/ppermute | solution.py:24
  19.3 10.5 %collective-permute-start.2 = (bf16[2,2,10,1,8,256]{5,4,3,2,1,0:T(8,128)(2,1)S(1)}, bf16[2,2,10,1,8,256]{5,4,3,2,1,0:T(8,128)(2,1)S(1)}, u32[]{:S(2)}, u32[]{:S(2)}) collective-permute-start(bf16[2,2,10,1,8,256]{5,4,3,2,1,0:T(8,128)(2,1)S(1)} %get-tuple-element.28), channel_id=1, source_target_pairs={{0,1},{1,2},{2,3},{4,5},{5,6},{6,7},{8,9},{9,10},{10,11},{12,13},{... | collective-permute-start | bytes 491528 | tf_op jit(solution)/shard_map/ppermute | solution.py:24
  23.5 6.6 %collective-permute-start.3 = (bf16[2,2,10,1,8,256]{5,4,3,2,1,0:T(8,128)(2,1)S(1)}, bf16[2,2,10,1,8,256]{5,4,3,2,1,0:T(8,128)(2,1)S(1)}, u32[]{:S(2)}, u32[]{:S(2)}) collective-permute-start(bf16[2,2,10,1,8,256]{5,4,3,2,1,0:T(8,128)(2,1)S(1)} %get-tuple-element.29), channel_id=1, source_target_pairs={{1,0},{2,1},{3,2},{5,4},{6,5},{7,6},{9,8},{10,9},{11,10},{13,12},{... | collective-permute-start | bytes 491528 | tf_op jit(solution)/shard_map/ppermute | solution.py:24

commit v2 on v1

v2 whole, which is shorter than its diff:
```python
import functools

import jax
import jax.numpy as jnp
from jax import lax
from jax.experimental import pallas as pl
from jax.experimental.pallas import tpu as pltpu
from jax.sharding import PartitionSpec as P

MESH = pl.DeviceIdType.MESH
VMEM = pltpu.VMEM
PARTS = 3
LANES = 128
UNITS_AFTER = (2, 1, 1, 0)
UNITS_BACK = (0, 1, 1, 0)


def shift_by_one(cells, axis):
    count = lax.axis_size(axis)
    ends = count - 1
    head = lambda dim: lax.slice_in_dim(cells, 0, 1, axis=dim)
    tail = lambda dim: lax.slice_in_dim(cells, cells.shape[dim] - 1, cells.shape[dim], axis=dim)
    up = [(i, i + 1) for i in range(ends)]
    down = [(i + 1, i) for i in range(ends)]
    return lambda dim: jnp.concatenate(
        [lax.ppermute(tail(dim), axis, up), cells, lax.ppermute(head(dim), axis, down)], axis=dim
    )


def spread(table, dim):
    first = lax.slice_in_dim(table, 0, 1, axis=dim)
    middle = lax.slice_in_dim(table, 1, 2, axis=dim)
    last = lax.slice_in_dim(table, 2, 3, axis=dim)
    return jnp.concatenate([first] + [middle] * 8 + [last], axis=dim)


def z_shifted(both, neighbors):
    slots = both.shape[1]
    wide = shift_by_one(both, "gx")(2)
    wide = shift_by_one(wide, "gy")(3)
    table = spread(spread(neighbors.reshape(slots, 3, 3, 3), 1), 2)

    def pick(layer, oz):
        total = None
        for slot in range(slots):
            hit = (table[:, :, :, oz] == slot)[None, :, :, :, None, None]
            part = jnp.where(hit, wide[:, slot : slot + 1, :, :, layer], jnp.zeros((), wide.dtype))
            total = part if total is None else total + part
        return total

    low = pick(slice(7, 8), 0)
    mid = pick(slice(0, 8), 1)
    high = pick(slice(0, 1), 2)
    return jnp.stack(
        [
            jnp.concatenate([low, mid[..., :7, :]], 4),
            mid,
            jnp.concatenate([mid[..., 1:, :], high], 4),
        ]
    )


def encode(values):
    peak = jnp.maximum(jnp.max(jnp.abs(values), axis=0, keepdims=True), 1e-33)
    return jnp.round(values * (32767.0 / peak)).astype(jnp.int32).astype(jnp.int16), peak * (1.0 / 32767.0)


def decode(code, unit):
    return code.astype(jnp.int32).astype(jnp.float32) * unit


def conv_kernel(plan, slots, scale, even_ref, odd_ref, w_ref, grad_t_ref, out_ref, back_ref, *rest):
    width = w_ref.shape[-1]

    def window(tensor, brick, ox, oy, oz):
        if oy == 1:
            value = odd_ref[oz, tensor, brick, ox : ox + 8]
        else:
            value = even_ref[oz, tensor, brick, ox : ox + 8, 8 * oy : 8 * oy + 64]
        return value.reshape(512, width)

    def grad_terms(ox, terms_ref):
        for oy in range(3):
            for oz in range(3):
                both = jnp.concatenate([window(0, brick, ox, oy, oz) for brick in range(slots)], 0)
                term = jnp.dot(grad_t_ref[...], both, preferred_element_type=jnp.float32)
                offset = 9 * ox + 3 * oy + oz
                terms_ref[offset * width : (offset + 1) * width] = term.T

    def features_unit(tensor, ox, acc):
        for oy in range(3):
            first = 9 * ox + 3 * oy
            if tensor == 0:
                rhs = w_ref[first : first + 3].reshape(3 * width, width)
            else:
                rhs = jnp.concatenate([w_ref[26 - first - oz] for oz in range(3)], 1)
            for brick in range(slots):
                rows = slice(512 * brick, 512 * brick + 512)
                lhs = jnp.concatenate([window(tensor, brick, ox, oy, oz) for oz in range(3)], 1)
                part = lax.dot_general(
                    lhs, rhs, (((1,), (tensor,)), ((), ())), preferred_element_type=jnp.float32
                )
                if ox == 0 and oy == 0:
                    acc[rows] = part
                else:
                    acc[rows] += part

    def units(accs):
        for tensor, acc, target in ((0, accs[0], out_ref), (1, accs[1], back_ref)):
            for ox in range(3):
                features_unit(tensor, ox, acc)
                if ox == 2:
                    target[...] = acc[...].astype(target.dtype)
                yield

    if plan is None:
        terms_ref, *accs = rest
        for ox in range(3):
            grad_terms(ox, terms_ref)
        for _ in units(accs):
            pass
        return

    pair, orders = plan
    stages = len(orders[0]) + 1
    code_out, unit_out, terms_ref, acc, *accs = rest[:6]
    buffers = rest[6 : 6 + 4 * stages]
    code_to, code_in, unit_to, unit_in = (buffers[i * stages : (i + 1) * stages] for i in range(4))
    send_sem, recv_sem = rest[6 + 4 * stages :]
    part_rows = acc.shape[1]
    block = part_rows >> (stages - 1)
    part_blocks = part_rows // block
    place = {"gx": lax.axis_index("gx"), "gy": lax.axis_index("gy")}

    def bit_of(bit):
        axis, step = bit
        return (place[axis] // step) % 2

    def partner(bit):
        axis, step = bit
        there = dict(place)
        there[axis] = place[axis] + step - 2 * step * bit_of(bit)
        return (there["gx"], there["gy"])

    barrier = pltpu.get_barrier_semaphore()
    for bit in [pair] + sorted(orders[0]):
        pl.semaphore_signal(barrier, inc=1, device_id=partner(bit), device_id_type=MESH)

    side = bit_of(pair)
    mine = pl.ds(pl.multiple_of(side * LANES, LANES), LANES)
    other = pl.ds(pl.multiple_of((1 - side) * LANES, LANES), LANES)
    started = []
    flying = [None] * PARTS

    def send(spans, step, part, bit):
        flying[part] = []
        for which, (src, dst) in enumerate(spans):
            copy = pltpu.make_async_remote_copy(
                src_ref=src,
                dst_ref=dst,
                send_sem=send_sem.at[step, part, which],
                recv_sem=recv_sem.at[step, part, which],
                device_id=partner(bit),
                device_id_type=MESH,
            )
            copy.start()
            started.append(copy)
            flying[part].append(copy)

    def arrived(part):
        for copy in flying[part]:
            copy.wait_recv()

    def rows_at(first):
        return pl.ds(pl.multiple_of(first, 16), block)

    def send_coded(stage, part, bit):
        send(
            [
                (code_to[stage].at[part], code_in[stage].at[part]),
                (unit_to[stage].at[part], unit_in[stage].at[part]),
            ],
            stage,
            part,
            bit,
        )

    work = units(accs)
    base = [0] * PARTS
    for p in range(PARTS):
        grad_terms(p, terms_ref)

        @pl.loop(0, part_blocks)
        def _(i):
            code, unit = encode(terms_ref[rows_at(p * part_rows + i * block), other])
            code_to[0][p, rows_at(i * block)] = code
            unit_to[0][p, i] = unit

        if p == 0:
            pl.semaphore_wait(barrier, stages)
        send_coded(0, p, pair)

    for stage in range(stages):
        blocks = part_blocks >> stage
        for p in range(PARTS):
            arrived(p)

            @pl.loop(0, blocks)
            def _(i):
                value = decode(code_in[stage][p, rows_at(i * block)], unit_in[stage][p, i])
                if stage == 0:
                    own = terms_ref[rows_at(p * part_rows + i * block), mine]
                else:
                    own = acc[p, rows_at((base[p] + i) * block)]
                acc[p, rows_at((base[p] + i) * block)] = own + value

            if stage < stages - 1:
                bit = orders[p][stage]
                half = blocks // 2
                away = base[p] + (1 - bit_of(bit)) * half
                base[p] = base[p] + bit_of(bit) * half

                @pl.loop(0, half)
                def _(i):
                    code, unit = encode(acc[p, rows_at((away + i) * block)])
                    code_to[stage + 1][p, rows_at(i * block)] = code
                    unit_to[stage + 1][p, i] = unit

                send_coded(stage + 1, p, bit)
            else:
                code, unit = encode(acc[p, rows_at(base[p] * block)] * scale)
                code_out[rows_at(p * part_rows + base[p] * block), mine] = code
                unit_out[side, p * part_blocks + base[p]] = unit
        for _ in range(UNITS_AFTER[stage] if stage < stages - 1 else 0):
            next(work, None)
        if stage < stages - 1:
            continue
        for p in range(PARTS):
            code_span = code_out.at[rows_at(p * part_rows + base[p] * block), mine]
            unit_span = unit_out.at[side, pl.ds(p * part_blocks + base[p], 1)]
            send([(code_span, code_span), (unit_span, unit_span)], stages, p, orders[p][-1])

    for back in range(1, stages + 1):
        level = stages - 1 - back
        for p in range(PARTS):
            arrived(p)
            if level < 0:
                continue
            blocks = part_blocks >> level
            base[p] = base[p] - bit_of(orders[p][level]) * (blocks // 2)
            first = pl.multiple_of(p * part_rows + base[p] * block, 16)
            code_span = code_out.at[pl.ds(first, blocks * block), mine]
            unit_span = unit_out.at[side, pl.ds(p * part_blocks + base[p], blocks)]
            bit = orders[p][level - 1] if level > 0 else pair
            send([(code_span, code_span), (unit_span, unit_span)], stages + back, p, bit)
        if level >= 0:
            for _ in range(UNITS_BACK[back - 1]):
                next(work, None)
    for _ in work:
        pass
    for copy in started:
        copy.wait_send()


def sum_plan(mesh, rows):
    sizes = dict(mesh.shape)
    if sizes["gx"] != 8 or sizes["gy"] != 4 or rows % (PARTS * 16 * 16):
        return None
    pair, x, y, z_near, z_far = ("gy", 1), ("gy", 2), ("gx", 1), ("gx", 2), ("gx", 4)
    return pair, [[x, y, z_near, z_far], [y, x, z_near, z_far], [z_near, z_far, x, y]]


def conv(plan, even, odd, weights, grad_t, scale):
    slots = even.shape[2]
    width = even.shape[-1]
    rows = slots * 512
    offsets = weights.shape[0]
    vmem = pl.BlockSpec(memory_space=VMEM)
    outs = [jax.ShapeDtypeStruct((rows, width), jnp.bfloat16)] * 2
    accs = [VMEM((rows, width), jnp.float32)] * 2
    full = (offsets * width, width)
    if plan is None:
        outs = outs + [jax.ShapeDtypeStruct(full, jnp.float32)]
        scratch = accs
        params = pltpu.CompilerParams(vmem_limit_bytes=58 * 2**20)
    else:
        stages = len(plan[1][0]) + 1
        part_rows = offsets * width // PARTS
        part_blocks = 1 << (stages - 1)
        outs = outs + [
            jax.ShapeDtypeStruct(full, jnp.int16),
            jax.ShapeDtypeStruct((2, PARTS * part_blocks, 1, LANES), jnp.float32),
        ]
        codes = [VMEM((PARTS, part_rows >> s, LANES), jnp.int16) for s in range(stages)]
        units = [VMEM((PARTS, part_blocks >> s, 1, LANES), jnp.float32) for s in range(stages)]
        sems = pltpu.SemaphoreType.DMA((2 * stages, PARTS, 2))
        scratch = (
            [VMEM(full, jnp.float32), VMEM((PARTS, part_rows, LANES), jnp.float32)]
            + accs
            + codes
            + codes
            + units
            + units
            + [sems, sems]
        )
        params = pltpu.CompilerParams(
            collective_id=0, has_side_effects=True, vmem_limit_bytes=58 * 2**20
        )
    return pl.pallas_call(
        functools.partial(conv_kernel, plan, slots, scale),
        in_specs=[vmem] * 4,
        out_specs=[vmem] * len(outs),
        out_shape=outs,
        scratch_shapes=scratch,
        compiler_params=params,
        cost_estimate=pl.CostEstimate(
            flops=offsets * 6 * rows * width * width, bytes_accessed=24 * 2**20, transcendentals=0
        ),
    )(even, odd, weights, grad_t)


def shards(plan, features, cotangent, kernel, occupancy, neighbors):
    slots = features.shape[0]
    width = features.shape[-1]
    mask_b = occupancy.reshape(slots, 8, 8, 8, 1).astype(jnp.bfloat16)
    masked = features * mask_b
    masked_grad = cotangent * mask_b
    both = jnp.stack([masked, masked_grad])
    shifted = z_shifted(both, neighbors)
    even = shifted.reshape(3, 2, slots, 10, 80, width)
    odd = shifted[:, :, :, :, 1:9].reshape(3, 2, slots, 10, 64, width)
    grad_t = masked_grad.reshape(-1, width).T
    scale = 1.0 / (512.0 * slots * lax.axis_size("gx") * lax.axis_size("gy")) ** 0.5
    if width != 2 * LANES:
        plan = None
    out, back, *total = conv(plan, even, odd, kernel, grad_t, scale)
    if plan is None:
        kernel_grad = lax.psum(total[0], ("gx", "gy")) * jnp.float32(scale)
    else:
        code, unit = total
        blocks = unit.shape[1]
        unit = unit.transpose(1, 2, 0, 3).reshape(blocks, 1, width)
        kernel_grad = decode(code.reshape(blocks, -1, width), unit)
    return (
        out.reshape(features.shape) * mask_b,
        back.reshape(features.shape) * mask_b,
        kernel_grad.reshape(kernel.shape),
    )


def solution(mesh):
    placed = (
        P(("gx", "gy"), None, None, None, None),
        P(("gx", "gy"), None, None, None, None),
        P(),
        P(("gx", "gy"), None),
        P(("gx", "gy"), None),
    )
    plan = sum_plan(mesh, 27 * 256)
    return jax.shard_map(
        functools.partial(shards, plan),
        mesh=mesh,
        in_specs=placed,
        out_specs=(
            P(("gx", "gy"), None, None, None, None),
            P(("gx", "gy"), None, None, None, None),
            P(),
        ),
        check_vma=False,
    )
```

time: 171 us -> 112 us (0.65)
  the two profiles are of different devices: /device:TPU:21 before, /device:TPU:1 now
where the time goes in v2:
time: 112 us; the launch traced here: 111 us
  Pallas kernels  64.7 us (58%)
  other arithmetic  23.9 us (21%)
  starting transfers between devices  12.3 us (11%)
  waiting for transfers between devices  5.02 us (4%)
  local copies, waits for them, and re-layouts  4.51 us (4%)
    pallas_call x1, Pallas kernels, conv(): pl.pallas_call(functools.partial(conv_kernel, plan, slots, scale), in_spe...  64.7 us
    ppermute x2, starting transfers between devices, shift_by_one(): lax.ppermute(tail(dim), axis, up)  9.09 us
    ppermute x2, waiting for transfers between devices, shift_by_one(): lax.ppermute(head(dim), axis, down)  5.01 us
    another operation x3, other arithmetic, z_shifted(): jnp.stack([jnp.concatenate([low, mid[..., :7, :]], 4), mid, jnp.concatena...  4.45 us
    mul x1, other arithmetic, decode(): return code.astype(jnp.int32).astype(jnp.float32) * unit  3.98 us
    add x4, other arithmetic, pick(): total = part if total is None else total + part  3.64 us
    ppermute x2, starting transfers between devices, shift_by_one(): lax.ppermute(head(dim), axis, down)  3.21 us
    convert_element_type x1, other arithmetic, decode(): return code.astype(jnp.int32).astype(jnp.float32) * unit  3 us
  transfers between devices with their start and end apart: 4, of which 2 were waited for; matrix products, arithmetic and copies ran while one was open for 4% of the time, Pallas kernels for 0%

profile of v2, /device:TPU:1, one launch (start us, length us, event | category | flops | bytes accessed | tf_op | source)
XLA Modules:
  0.0 111.4 jit_solution(5961712981287842508)
XLA Ops:
  0.6 0.7 convert_element_type.23
  1.4 1.4 %multiply_bitcast_fusion = (bf16[1,2,8,8,8,256]{5,4,3,2,1,0:T(8,128)(2,1)S(1)}, bf16[2,8,8,8,256]{4,3,2,1,0:T(8,128)(2,1)S(1)}) fusion(bf16[2,8,8,8,256]{4,3,2,1,0:T(8,128)(2,1)} %param.5, bf16[2,8,8,8]{3,2,1,0:T(8,128)(2,1)S(1)} %convert_element_type.24, bf16[2,8,8,8,256]{4,3,2,1,0:T(8,128)(2,1)} %param.6), kind=kLoop, calls=%fused_computation.23 | loop fusion | flops 524288 | bytes 2099200 | tf_op jit(solution)/shard_map/stack | solution.py:328
  2.9 4.0 %collective-permute-start = (bf16[2,2,1,8,8,256]{5,4,3,2,1,0:T(8,128)(2,1)S(1)}, bf16[2,2,1,8,8,256]{5,4,3,2,1,0:T(8,128)(2,1)S(1)}, u32[]{:S(2)}, u32[]{:S(2)}) collective-permute-start(bf16[2,2,1,8,8,256]{5,4,3,2,1,0:T(8,128)(2,1)S(1)} %get-tuple-element.32), channel_id=1, source_target_pairs={{0,4},{4,8},{8,12},{12,16},{16,20},{20,24},{24,28},{1,5},{5,9},{9,... | collective-permute-start | bytes 393224 | tf_op jit(solution)/shard_map/ppermute | solution.py:26
  6.9 1.3 %collective-permute-start.1 = (bf16[2,2,1,8,8,256]{5,4,3,2,1,0:T(8,128)(2,1)S(1)}, bf16[2,2,1,8,8,256]{5,4,3,2,1,0:T(8,128)(2,1)S(1)}, u32[]{:S(2)}, u32[]{:S(2)}) collective-permute-start(bf16[2,2,1,8,8,256]{5,4,3,2,1,0:T(8,128)(2,1)S(1)} %get-tuple-element.33), channel_id=1, source_target_pairs={{4,0},{8,4},{12,8},{16,12},{20,16},{24,20},{28,24},{5,1},{9,5},{13... | collective-permute-start | bytes 393224 | tf_op jit(solution)/shard_map/ppermute | solution.py:26
  8.4 0.1 concatenate.22
  8.5 2.2 %compare_reduce_fusion.4 = (pred[2,10,10]{2,1,0:T(8,128)(4,1)S(1)}, pred[2,10,10]{2,1,0:T(8,128)(4,1)S(1)}, pred[2,10,10]{2,1,0:T(8,128)(4,1)S(1)}, pred[2,10,10...) fusion(s32[2,10,10,3]{3,2,1,0:T(8,128)S(1)} %concatenate.22), kind=kLoop, calls=%fused_computation.41 | loop fusion | flops 1200 | bytes 3600 | tf_op jit(solution)/shard_map/eq | solution.py:46
  10.8 0.1 copy.87
  10.9 0.1 copy.85
  11.2 1.4 %collective-permute-done.1 = bf16[2,2,1,8,8,256]{5,4,3,2,1,0:T(8,128)(2,1)S(1)} collective-permute-done((bf16[2,2,1,8,8,256]{5,4,3,2,1,0:T(8,128)(2,1)S(1)}, bf16[2,2,1,8,8,256]{5,4,3,2,1,0:T(8,128)(2,1)S(1)}, u32[]{:S(2)}, u32[]{:S(2)}) %collective-permute-start.1) | collective-permute-done | bytes 131104 | tf_op jit(solution)/shard_map/ppermute | solution.py:26
  12.6 5.1 %collective-permute-start.2 = (bf16[2,2,10,1,8,256]{5,4,3,2,1,0:T(8,128)(2,1)S(1)}, bf16[2,2,10,1,8,256]{5,4,3,2,1,0:T(8,128)(2,1)S(1)}, u32[]{:S(2)}, u32[]{:S(2)}) collective-permute-start(bf16[2,2,10,1,8,256]{5,4,3,2,1,0:T(8,128)(2,1)S(1)} %get-tuple-element.30), channel_id=1, source_target_pairs={{0,1},{1,2},{2,3},{4,5},{5,6},{6,7},{8,9},{9,10},{10,11},{12,13},{... | collective-permute-start | bytes 491528 | tf_op jit(solution)/shard_map/ppermute | solution.py:26
  17.8 1.9 %collective-permute-start.3 = (bf16[2,2,10,1,8,256]{5,4,3,2,1,0:T(8,128)(2,1)S(1)}, bf16[2,2,10,1,8,256]{5,4,3,2,1,0:T(8,128)(2,1)S(1)}, u32[]{:S(2)}, u32[]{:S(2)}) collective-permute-start(bf16[2,2,10,1,8,256]{5,4,3,2,1,0:T(8,128)(2,1)S(1)} %get-tuple-element.31), channel_id=1, source_target_pairs={{1,0},{2,1},{3,2},{5,4},{6,5},{7,6},{9,8},{10,9},{11,10},{13,12},{... | collective-permute-start | bytes 491528 | tf_op jit(solution)/shard_map/ppermute | solution.py:26
  19.8 1.0 copy.93
  20.8 3.6 %collective-permute-done.3 = bf16[2,2,10,1,8,256]{5,4,3,2,1,0:T(8,128)(2,1)S(1)} collective-permute-done((bf16[2,2,10,1,8,256]{5,4,3,2,1,0:T(8,128)(2,1)S(1)}, bf16[2,2,10,1,8,256]{5,4,3,2,1,0:T(8,128)(2,1)S(1)}, u32[]{:S(2)}, u32[]{:S(2)}) %collective-permute-start.3) | collective-permute-done | bytes 163872 | tf_op jit(solution)/shard_map/ppermute | solution.py:26
  24.4 0.3 pad_maximum_fusion.3
  24.7 0.2 slice_bitcast_fusion.2
  25.0 0.8 select_add_fusion
  25.8 0.6 select_add_fusion.2
  26.4 0.2 pad_maximum_fusion.8
  26.8 0.5 pad_maximum_fusion.9
  27.8 0.5 fusion.7
  28.3 1.6 %fusion.5 = (bf16[2,2,10,10,1,256]{5,4,3,2,1,0:T(2,128)(2,1)S(1)}, bf16[2,2,10,10,1,256]{5,4,3,2,1,0:T(2,128)(2,1)S(1)}) fusion(pred[2,10,10]{2,1,0:T(8,128)(4,1)S(1)} %get-tuple-element.16, pred[2,10,10]{2,1,0:T(8,128)(4,1)S(1)} %get-tuple-element.11, bf16[2,10,10,256]{3,2,1,0:T(8,128)(2,1)S(1)} %copy.84, bf16[2,10,10,256]{3,2,1,0:T(8,128)(2,1)S(1)} %copy.82, ...), kind=kLoop, calls=%fused_computation.24 | loop fusion | flops 614400 | bytes 820000 | tf_op jit(solution)/shard_map/add | solution.py:48
  29.9 0.8 fusion.3
  30.7 0.8 fusion.1
  31.6 2.1 %fusion.odd_ref = bf16[3,2,2,10,64,256]{5,4,3,2,1,0:T(8,128)(2,1)} fusion(bf16[1,2,2,10,10,8,256]{6,5,4,3,2,1,0:T(8,128)(2,1)S(1)} %get-tuple-element.19, bf16[1,2,2,10,10,8,256]{6,5,4,3,2,1,0:T(8,128)(2,1)S(1)} %select_add_fusion, bf16[1,2,2,10,10,8,256]{6,5,4,3,2,1,0:T(8,128)(2,1)S(1)} %get-tuple-element.17), kind=kLoop, calls=%fused_computation.3 | loop fusion | flops 3932160 | bytes 8847360 | tf_op jit(solution)/shard_map/reshape | solution.py:331
  33.7 0.6 select_add_fusion.1
  34.3 2.8 %pad_maximum_fusion.even_ref = bf16[3,2,2,10,80,256]{5,4,3,2,1,0:T(8,128)(2,1)} fusion(bf16[1,2,2,10,80,256]{5,4,3,2,1,0:T(8,128)(2,1)S(1)} %get-tuple-element.20, bf16[1,2,2,10,80,256]{5,4,3,2,1,0:T(8,128)(2,1)S(1)} %select_add_fusion.1, bf16[1,2,2,10,80,256]{5,4,3,2,1,0:T(8,128)(2,1)S(1)} %get-tuple-element.18), kind=kLoop, calls=%fused_computation.1 | loop fusion | flops 4915200 | bytes 9830400 | tf_op jit(solution)/shard_map/stack | solution.py:54
  37.1 64.7 %shard_map.76 = (bf16[1024,256]{1,0:T(8,128)(2,1)}, bf16[1024,256]{1,0:T(8,128)(2,1)}, s16[6912,256]{1,0:T(8,128)(2,1)}, f32[2,48,1,128]{3,2,1,0:T(1,128)}) custom-call(bf16[3,2,2,10,80,256]{5,4,3,2,1,0:T(8,128)(2,1)} %pad_maximum_fusion.even_ref, bf16[3,2,2,10,64,256]{5,4,3,2,1,0:T(8,128)(2,1)} %fusion.odd_ref, bf16[27,256,256]{2,1,0:T(8,128)(2,1)} %w_ref.1, ...), custom_call_target="tpu_custom_call" | custom-call | flops 10871635968 | bytes 25165824 | tf_op jit(solution)/shard_map/pallas_call | solution.py:309
  101.8 0.8 copy.94
  102.6 3.0 %convert_convert_fusion = f32[6912,256]{1,0:T(8,128)S(1)} fusion(s16[6912,256]{1,0:T(8,128)(2,1)} %get-tuple-element.9), kind=kLoop, calls=%fused_computation | loop fusion | flops 3538944 | bytes 10616832 | tf_op jit(solution)/shard_map/convert_element_type | solution.py:69
  105.7 1.2 %broadcast_multiply_fusion = (bf16[2,8,8,8,256]{4,3,2,1,0:T(8,128)(2,1)}, bf16[2,8,8,8,256]{4,3,2,1,0:T(8,128)(2,1)}) fusion(bf16[2,8,8,8,256]{4,3,2,1,0:T(8,128)(2,1)S(1)} %bitcast.60, bf16[2,8,8,8]{3,2,1,0:T(8,128)(2,1)S(1)} %convert_element_type.24, bf16[2,8,8,8,256]{4,3,2,1,0:T(8,128)(2,1)S(1)} %bitcast.59), kind=kLoop, calls=%fused_computation.26 | loop fusion | flops 524288 | bytes 2099200 | tf_op jit(solution)/shard_map/mul | solution.py:346
  106.8 0.5 mul.45
  107.4 4.0 %mul.47 = f32[27,256,256]{2,1,0:T(8,128)} multiply(f32[27,256,256]{2,1,0:T(8,128)S(1)} %bitcast.50, f32[27,256,256]{2,1,0:T(8,128)S(1)} %bitcast.51) | non-fusion elementwise | flops 1769472 | bytes 21233664 | tf_op jit(solution)/shard_map/mul | solution.py:69
  (35 shorter events, 1.1 us)
Async XLA Ops:
  1.4 6.7 %copy-start.2 = (s32[2,27]{1,0:T(2,128)S(1)}, s32[2,27]{1,0:T(2,128)}, u32[]{:S(2)}) copy-start(s32[2,27]{1,0:T(2,128)} %param.9) | copy-start | bytes 652
  2.9 8.3 %collective-permute-start = (bf16[2,2,1,8,8,256]{5,4,3,2,1,0:T(8,128)(2,1)S(1)}, bf16[2,2,1,8,8,256]{5,4,3,2,1,0:T(8,128)(2,1)S(1)}, u32[]{:S(2)}, u32[]{:S(2)}) collective-permute-start(bf16[2,2,1,8,8,256]{5,4,3,2,1,0:T(8,128)(2,1)S(1)} %get-tuple-element.32), channel_id=1, source_target_pairs={{0,4},{4,8},{8,12},{12,16},{16,20},{20,24},{24,28},{1,5},{5,9},{9,... | collective-permute-start | bytes 393224 | tf_op jit(solution)/shard_map/ppermute | solution.py:26
  6.9 5.7 %collective-permute-start.1 = (bf16[2,2,1,8,8,256]{5,4,3,2,1,0:T(8,128)(2,1)S(1)}, bf16[2,2,1,8,8,256]{5,4,3,2,1,0:T(8,128)(2,1)S(1)}, u32[]{:S(2)}, u32[]{:S(2)}) collective-permute-start(bf16[2,2,1,8,8,256]{5,4,3,2,1,0:T(8,128)(2,1)S(1)} %get-tuple-element.33), channel_id=1, source_target_pairs={{4,0},{8,4},{12,8},{16,12},{20,16},{24,20},{28,24},{5,1},{9,5},{13... | collective-permute-start | bytes 393224 | tf_op jit(solution)/shard_map/ppermute | solution.py:26
  12.6 8.2 %collective-permute-start.2 = (bf16[2,2,10,1,8,256]{5,4,3,2,1,0:T(8,128)(2,1)S(1)}, bf16[2,2,10,1,8,256]{5,4,3,2,1,0:T(8,128)(2,1)S(1)}, u32[]{:S(2)}, u32[]{:S(2)}) collective-permute-start(bf16[2,2,10,1,8,256]{5,4,3,2,1,0:T(8,128)(2,1)S(1)} %get-tuple-element.30), channel_id=1, source_target_pairs={{0,1},{1,2},{2,3},{4,5},{5,6},{6,7},{8,9},{9,10},{10,11},{12,13},{... | collective-permute-start | bytes 491528 | tf_op jit(solution)/shard_map/ppermute | solution.py:26
  17.8 6.6 %collective-permute-start.3 = (bf16[2,2,10,1,8,256]{5,4,3,2,1,0:T(8,128)(2,1)S(1)}, bf16[2,2,10,1,8,256]{5,4,3,2,1,0:T(8,128)(2,1)S(1)}, u32[]{:S(2)}, u32[]{:S(2)}) collective-permute-start(bf16[2,2,10,1,8,256]{5,4,3,2,1,0:T(8,128)(2,1)S(1)} %get-tuple-element.31), channel_id=1, source_target_pairs={{1,0},{2,1},{3,2},{5,4},{6,5},{7,6},{9,8},{10,9},{11,10},{13,12},{... | collective-permute-start | bytes 491528 | tf_op jit(solution)/shard_map/ppermute | solution.py:26
  102.6 3.0 %copy-start = (bf16[1024,256]{1,0:T(8,128)(2,1)S(1)}, bf16[1024,256]{1,0:T(8,128)(2,1)}, u32[]{:S(2)}) copy-start(bf16[1024,256]{1,0:T(8,128)(2,1)} %get-tuple-element.7) | copy-start | bytes 1572868
  102.6 3.0 %copy-start.1 = (bf16[1024,256]{1,0:T(8,128)(2,1)S(1)}, bf16[1024,256]{1,0:T(8,128)(2,1)}, u32[]{:S(2)}) copy-start(bf16[1024,256]{1,0:T(8,128)(2,1)} %get-tuple-element.8) | copy-start | bytes 1572868

commit v3 on v2

--- a/solution.py
+++ b/solution.py
@@ -11,6 +11,7 @@
 VMEM = pltpu.VMEM
 PARTS = 3
 LANES = 128
+HALO = ((-1, 0), (1, 0), (0, -1), (0, 1), (-1, -1), (-1, 1), (1, -1), (1, 1))
 UNITS_AFTER = (2, 1, 1, 0)
 UNITS_BACK = (0, 1, 1, 0)
 
@@ -69,7 +70,11 @@
     return code.astype(jnp.int32).astype(jnp.float32) * unit
 
 
-def conv_kernel(plan, slots, scale, even_ref, odd_ref, w_ref, grad_t_ref, out_ref, back_ref, *rest):
+def conv_kernel(plan, slots, scale, *refs):
+    if plan is None:
+        even_ref, odd_ref, w_ref, grad_t_ref, out_ref, back_ref, *rest = refs
+    else:
+        both_ref, y_ref, corner_ref, near_ref, w_ref, grad_t_ref, out_ref, back_ref, *rest = refs
     width = w_ref.shape[-1]
 
     def window(tensor, brick, ox, oy, oz):
@@ -126,7 +131,8 @@
     code_out, unit_out, terms_ref, acc, *accs = rest[:6]
     buffers = rest[6 : 6 + 4 * stages]
     code_to, code_in, unit_to, unit_in = (buffers[i * stages : (i + 1) * stages] for i in range(4))
-    send_sem, recv_sem = rest[6 + 4 * stages :]
+    send_sem, recv_sem, even_ref, odd_ref, *halo = rest[6 + 4 * stages :]
+    halo_x, halo_y, halo_corner, edge_y, halo_send, halo_recv = halo
     part_rows = acc.shape[1]
     block = part_rows >> (stages - 1)
     part_blocks = part_rows // block
@@ -145,6 +151,121 @@
     barrier = pltpu.get_barrier_semaphore()
     for bit in [pair] + sorted(orders[0]):
         pl.semaphore_signal(barrier, inc=1, device_id=partner(bit), device_id_type=MESH)
+
+    def inside(sign, step):
+        col_x, col_y = place["gx"] + sign * step[0], place["gy"] + sign * step[1]
+        x_in = (col_x >= 0) & (col_x < lax.axis_size("gx"))
+        return x_in & (col_y >= 0) & (col_y < lax.axis_size("gy"))
+
+    def halo_copy(slot, sign):
+        step = HALO[slot]
+        low_x, low_y = int(step[0] > 0), int(step[1] > 0)
+        if step[1] == 0:
+            src, dst = both_ref.at[:, :, 0 if low_x else 7], halo_x.at[low_x]
+        elif step[0] == 0:
+            src, dst = y_ref.at[1 - low_y], halo_y.at[low_y]
+        else:
+            src, dst = corner_ref.at[1 - low_x, 1 - low_y], halo_corner.at[low_x, low_y]
+        there = (place["gx"] + sign * step[0], place["gy"] + sign * step[1])
+        return dst, pltpu.make_async_remote_copy(
+            src_ref=src,
+            dst_ref=dst,
+            send_sem=halo_send.at[slot],
+            recv_sem=halo_recv.at[slot],
+            device_id=there,
+            device_id_type=MESH,
+        )
+
+    near = stages
+    for slot, step in enumerate(HALO):
+        near = near + inside(1, step).astype(jnp.int32)
+
+        @pl.when(inside(-1, step))
+        def _():
+            there = (place["gx"] - step[0], place["gy"] - step[1])
+            pl.semaphore_signal(barrier, inc=1, device_id=there, device_id_type=MESH)
+
+    pl.semaphore_wait(barrier, near)
+    for slot, step in enumerate(HALO):
+        @pl.when(inside(-1, step))
+        def _():
+            halo_copy(slot, -1)[1].start()
+
+    height = lax.broadcasted_iota(jnp.int32, (1, 8, width), 1)
+
+    def extended_z(sources, brick, first):
+        def pick(offset):
+            slot_row = near_ref[brick * 27 + first + offset]
+            total = jnp.zeros_like(sources[0])
+            for slot in range(slots):
+                total = jnp.where(slot_row[None] == slot, sources[slot], total)
+            return total
+
+        low, mid, high = pick(0), pick(1), pick(2)
+        return [
+            pltpu.roll(jnp.where(height == 7, low, mid), 1, 1),
+            mid,
+            pltpu.roll(jnp.where(height == 0, high, mid), 7, 1),
+        ]
+
+    def cells(value):
+        return value.astype(jnp.float32).reshape(-1, 8, width)
+
+    def rows_of(value):
+        return value.reshape(-1, width).astype(jnp.bfloat16)
+
+    @pl.loop(0, 2 * slots)
+    def _(i):
+        tensor, brick = i // slots, i % slots
+
+        @pl.loop(0, 8)
+        def _(x):
+            sources = [cells(both_ref[tensor, slot, x]) for slot in range(slots)]
+            for oz, value in enumerate(extended_z(sources, brick, 12)):
+                odd_ref[oz, tensor, brick, x + 1] = rows_of(value)
+
+    for slot, step in enumerate(HALO):
+        dst, arriving = halo_copy(slot, 1)
+
+        @pl.when(inside(1, step))
+        def _():
+            arriving.wait_recv()
+
+        @pl.when(jnp.logical_not(inside(1, step)))
+        def _():
+            dst[...] = jnp.zeros(dst.shape, dst.dtype)
+
+    @pl.loop(0, 2 * slots)
+    def _(i):
+        tensor, brick = i // slots, i % slots
+        for end in range(2):
+            sources = [cells(halo_y[end, tensor, slot]) for slot in range(slots)]
+            for oz, value in enumerate(extended_z(sources, brick, 9 + 6 * end)):
+                edge_y[oz, end] = value
+
+        @pl.loop(0, 8)
+        def _(x):
+            for oz in range(3):
+                middle = cells(odd_ref[oz, tensor, brick, x + 1])
+                row = jnp.concatenate([edge_y[oz, 0, pl.ds(x, 1)], middle, edge_y[oz, 1, pl.ds(x, 1)]], 0)
+                even_ref[oz, tensor, brick, x + 1] = rows_of(row)
+
+        for end in range(2):
+            first = 18 * end
+            middle = extended_z(
+                [cells(halo_x[end, tensor, slot]) for slot in range(slots)], brick, first + 3
+            )
+            ends = []
+            for end_y in range(2):
+                column = [
+                    halo_corner[end, end_y, tensor, slot].astype(jnp.float32)[None, :8]
+                    for slot in range(slots)
+                ]
+                ends.append(extended_z(column, brick, first + 6 * end_y))
+            for oz in range(3):
+                row = jnp.concatenate([ends[0][oz], middle[oz], ends[1][oz]], 0)
+                even_ref[oz, tensor, brick, 9 * end] = rows_of(row)
+                odd_ref[oz, tensor, brick, 9 * end] = rows_of(middle[oz])
 
     side = bit_of(pair)
     mine = pl.ds(pl.multiple_of(side * LANES, LANES), LANES)
@@ -196,8 +317,6 @@
             code_to[0][p, rows_at(i * block)] = code
             unit_to[0][p, i] = unit
 
-        if p == 0:
-            pl.semaphore_wait(barrier, stages)
         send_coded(0, p, pair)
 
     for stage in range(stages):
@@ -260,6 +379,10 @@
         pass
     for copy in started:
         copy.wait_send()
+    for slot, step in enumerate(HALO):
+        @pl.when(inside(-1, step))
+        def _():
+            halo_copy(slot, -1)[1].wait_send()
 
 
 def sum_plan(mesh, rows):
@@ -270,9 +393,9 @@
     return pair, [[x, y, z_near, z_far], [y, x, z_near, z_far], [z_near, z_far, x, y]]
 
 
-def conv(plan, even, odd, weights, grad_t, scale):
-    slots = even.shape[2]
-    width = even.shape[-1]
+def conv(plan, slots, scale, *operands):
+    weights = operands[-2]
+    width = weights.shape[-1]
     rows = slots * 512
     offsets = weights.shape[0]
     vmem = pl.BlockSpec(memory_space=VMEM)
@@ -302,13 +425,18 @@
             + units
             + units
             + [sems, sems]
+            + [VMEM((3, 2, slots, 10, wide, width), jnp.bfloat16) for wide in (80, 64)]
+            + [VMEM((2, 2, slots, 64, width), jnp.bfloat16)] * 2
+            + [VMEM((2, 2, 2, slots, 16, width), jnp.bfloat16)]
+            + [VMEM((3, 2, 8, 8, width), jnp.float32)]
+            + [pltpu.SemaphoreType.DMA((8,))] * 2
         )
         params = pltpu.CompilerParams(
             collective_id=0, has_side_effects=True, vmem_limit_bytes=58 * 2**20
         )
     return pl.pallas_call(
         functools.partial(conv_kernel, plan, slots, scale),
-        in_specs=[vmem] * 4,
+        in_specs=[vmem] * len(operands),
         out_specs=[vmem] * len(outs),
         out_shape=outs,
         scratch_shapes=scratch,
@@ -316,7 +444,31 @@
         cost_estimate=pl.CostEstimate(
             flops=offsets * 6 * rows * width * width, bytes_accessed=24 * 2**20, transcendentals=0
         ),
-    )(even, odd, weights, grad_t)
+    )(*operands)
+
+
+def decode_kernel(code_ref, unit_ref, out_ref):
+    steps = unit_ref.shape[1]
+    block = code_ref.shape[0] // steps
+    for i in range(steps):
+        for side in range(2):
+            at = slice(i * block, (i + 1) * block), slice(side * LANES, (side + 1) * LANES)
+            out_ref[at] = decode(code_ref[at], unit_ref[side, i])
+
+
+def decode_all(code, unit):
+    rows, width = code.shape
+    steps = 8
+    tile = pl.BlockSpec((rows // steps, width), lambda i: (i, 0))
+    return pl.pallas_call(
+        decode_kernel,
+        grid=(steps,),
+        in_specs=[tile, pl.BlockSpec((2, unit.shape[1] // steps, 1, LANES), lambda i: (0, i, 0, 0))],
+        out_specs=tile,
+        out_shape=jax.ShapeDtypeStruct(code.shape, jnp.float32),
+        compiler_params=pltpu.CompilerParams(vmem_limit_bytes=24 * 2**20),
+        cost_estimate=pl.CostEstimate(flops=2 * rows * width, bytes_accessed=6 * rows * width, transcendentals=0),
+    )(code, unit)
 
 
 def shards(plan, features, cotangent, kernel, occupancy, neighbors):
@@ -326,21 +478,26 @@
     masked = features * mask_b
     masked_grad = cotangent * mask_b
     both = jnp.stack([masked, masked_grad])
-    shifted = z_shifted(both, neighbors)
-    even = shifted.reshape(3, 2, slots, 10, 80, width)
-    odd = shifted[:, :, :, :, 1:9].reshape(3, 2, slots, 10, 64, width)
     grad_t = masked_grad.reshape(-1, width).T
     scale = 1.0 / (512.0 * slots * lax.axis_size("gx") * lax.axis_size("gy")) ** 0.5
     if width != 2 * LANES:
         plan = None
-    out, back, *total = conv(plan, even, odd, kernel, grad_t, scale)
+    if plan is None:
+        shifted = z_shifted(both, neighbors)
+        even = shifted.reshape(3, 2, slots, 10, 80, width)
+        odd = shifted[:, :, :, :, 1:9].reshape(3, 2, slots, 10, 64, width)
+        operands = even, odd
+    else:
+        sides = jnp.stack([both[:, :, :, 0], both[:, :, :, 7]])
+        corners = jnp.stack([sides[:, :, :, 0], sides[:, :, :, 7]])
+        corners = jnp.concatenate([corners, jnp.zeros_like(corners)], -2)
+        near = jnp.broadcast_to(neighbors.reshape(-1, 1, 1), (neighbors.size, 1, width))
+        operands = both.reshape(2, slots, 8, 64, width), sides.reshape(2, 2, slots, 64, width), corners, near
+    out, back, *total = conv(plan, slots, scale, *operands, kernel, grad_t)
     if plan is None:
         kernel_grad = lax.psum(total[0], ("gx", "gy")) * jnp.float32(scale)
     else:
-        code, unit = total
-        blocks = unit.shape[1]
-        unit = unit.transpose(1, 2, 0, 3).reshape(blocks, 1, width)
-        kernel_grad = decode(code.reshape(blocks, -1, width), unit)
+        kernel_grad = decode_all(*total)
     return (
         out.reshape(features.shape) * mask_b,
         back.reshape(features.shape) * mask_b,

time: 112 us -> 91.9 us (0.82)
  other arithmetic: 23.9 us -> 6.14 us
  Pallas kernels: 64.7 us -> 80.4 us
  starting transfers between devices: 12.3 us -> 0 us
  waiting for transfers between devices: 5.02 us -> 0 us
    ppermute x4 -> x0, starting transfers between devices: 12.3 us -> none  [the longest x2 9.09 us: shift_by_one(): lax.ppermute(tail(dim), axis, up)]
    pallas_call x1, Pallas kernels: 64.7 us -> 76.1 us  [conv(): pl.pallas_call(functools.partial(conv_kernel, plan, slots, scale), in_spe...]
    ppermute x4 -> x0, waiting for transfers between devices: 5.02 us -> none  [the longest x2 5.01 us: shift_by_one(): lax.ppermute(head(dim), axis, down)]
    pallas_call x0 -> x1, Pallas kernels: none -> 4.29 us  [decode_all(): pl.pallas_call(decode_kernel, grid=(steps,), in_specs=[tile, pl.BlockSpec...]
    add x4 -> x0, other arithmetic: 3.64 us -> none  [pick(): total = part if total is None else total + part]
    another operation x3, other arithmetic: 4.45 us -> 1.4 us  [the longest x1 0.73 us: shards(): sides = jnp.stack([both[:, :, :, 0], both[:, :, :, 7]])]
    convert_element_type x1 -> x0, other arithmetic: 3 us -> none  [decode(): return code.astype(jnp.int32).astype(jnp.float32) * unit]
    mul x1, other arithmetic: 3.98 us -> 1.4 us  [shards(): masked = features * mask_b]
  transfers between devices with their start and end apart: 4 -> 0, of which waited for: 2 -> 0; matrix products, arithmetic and copies ran while one was open for 4% -> 0% of each run, Pallas kernels for 0% -> 0%
where the time goes in v3:
time: 91.9 us; the launch traced here: 91.7 us
  Pallas kernels  80.4 us (87%)
  other arithmetic  6.14 us (7%)
  local copies, waits for them, and re-layouts  4.44 us (5%)
    pallas_call x1, Pallas kernels, conv(): pl.pallas_call(functools.partial(conv_kernel, plan, slots, scale), in_spe...  76.1 us
    pallas_call x1, Pallas kernels, decode_all(): pl.pallas_call(decode_kernel, grid=(steps,), in_specs=[tile, pl.BlockSpec...  4.29 us

profile of v3, /device:TPU:1, one launch (start us, length us, event | category | flops | bytes accessed | tf_op | source)
XLA Modules:
  0.0 91.7 jit_solution(10480252084751729651)
XLA Ops:
  0.6 0.8 broadcast_in_dim.8
  1.4 0.7 convert_element_type.11
  2.1 0.1 convert_element_type.12
  2.2 0.7 broadcast_in_dim.9.refs_3_
  3.0 1.4 %copy_multiply_fusion.3 = (bf16[2,8,8,8,256]{4,3,0,1,2:T(8,128)(2,1)S(1)}, bf16[2,8,8,8,256]{4,3,0,1,2:T(8,128)(2,1)S(1)}) fusion(bf16[2,8,8,8,256]{4,3,2,1,0:T(8,128)(2,1)} %param.5, bf16[2,8,8,8]{3,0,1,2:T(2,128)(2,1)S(1)} %copy.16, bf16[2,8,8,8,256]{4,3,2,1,0:T(8,128)(2,1)} %param.6), kind=kLoop, calls=%fused_computation.5 | loop fusion | flops 524288 | bytes 2099200 | tf_op jit(solution)/shard_map/mul | solution.py:478
  4.4 0.7 fusion.2.refs_2_
  5.1 0.7 pad_maximum_fusion.1.refs_1_
  5.9 1.0 %copy.26 = bf16[1024,256]{0,1:T(8,128)(2,1)} copy(bf16[1024,256]{1,0:T(8,128)(2,1)S(1)} %bitcast.29) | data formatting | bytes 1048576 | tf_op jit(solution)/shard_map/reshape | solution.py:481
  6.9 1.1 %pad_maximum_fusion.refs_0_ = bf16[2,2,8,64,256]{4,3,2,1,0:T(8,128)(2,1)} fusion(bf16[1,2,8,64,256]{4,3,2,1,0:T(8,128)(2,1)S(1)} %bitcast.30, bf16[1,2,8,64,256]{4,3,2,1,0:T(8,128)(2,1)S(1)} %bitcast.31), kind=kLoop, calls=%fused_computation | loop fusion | flops 524288 | bytes 2097152 | tf_op jit(solution)/shard_map/stack | solution.py:480
  8.0 76.1 %shard_map.76 = (bf16[1024,256]{1,0:T(8,128)(2,1)}, bf16[1024,256]{1,0:T(8,128)(2,1)}, s16[6912,256]{1,0:T(8,128)(2,1)}, f32[2,48,1,128]{3,2,1,0:T(1,128)}) custom-call(bf16[2,2,8,64,256]{4,3,2,1,0:T(8,128)(2,1)} %pad_maximum_fusion.refs_0_, bf16[2,2,2,64,256]{4,3,2,1,0:T(8,128)(2,1)} %pad_maximum_fusion.1.refs_1_, ...), custom_call_target="tpu_custom_call" | custom-call | flops 10871635968 | bytes 25165824 | tf_op jit(solution)/shard_map/pallas_call | solution.py:437
  84.2 0.0 copy-start
  84.2 0.0 copy-start.1
  84.2 1.6 %copy_multiply_fusion = (bf16[2,8,8,8,256]{4,3,0,1,2:T(8,128)(2,1)S(1)}, bf16[2,8,8,8,256]{4,3,0,1,2:T(8,128)(2,1)S(1)}) fusion(bf16[2,8,8,8,256]{4,3,2,1,0:T(8,128)(2,1)} %bitcast.36, bf16[2,8,8,8]{3,0,1,2:T(2,128)(2,1)S(1)} %copy.16, bf16[2,8,8,8,256]{4,3,2,1,0:T(8,128)(2,1)} %bitcast.35), kind=kLoop, calls=%fused_computation.1 | loop fusion | flops 524288 | bytes 2099200 | tf_op jit(solution)/shard_map/mul | solution.py:503
  85.7 0.8 copy.30
  86.6 0.8 copy.29
  87.4 0.0 copy-done
  87.4 0.0 copy-done.1
  87.4 4.3 %shard_map.77 = f32[6912,256]{1,0:T(8,128)} custom-call(s16[6912,256]{1,0:T(8,128)(2,1)S(1)} %copy-done, f32[2,48,1,128]{3,2,1,0:T(1,128)S(1)} %copy-done.1), custom_call_target="tpu_custom_call" | custom-call | flops 3538944 | bytes 10616832 | tf_op jit(solution)/shard_map/pallas_call | solution.py:463
  (6 shorter events, 0.2 us)
Async XLA Ops:
  84.2 3.3 %copy-start = (s16[6912,256]{1,0:T(8,128)(2,1)S(1)}, s16[6912,256]{1,0:T(8,128)(2,1)}, u32[]{:S(2)}) copy-start(s16[6912,256]{1,0:T(8,128)(2,1)} %get-tuple-element.9.code_ref) | copy-start | bytes 10616836
  84.2 3.3 %copy-start.1 = (f32[2,48,1,128]{3,2,1,0:T(1,128)S(1)}, f32[2,48,1,128]{3,2,1,0:T(1,128)}, u32[]{:S(2)}) copy-start(f32[2,48,1,128]{3,2,1,0:T(1,128)} %get-tuple-element.10.unit_ref) | copy-start | bytes 147460

commit v4 on v3

--- a/solution.py
+++ b/solution.py
@@ -12,8 +12,8 @@
 PARTS = 3
 LANES = 128
 HALO = ((-1, 0), (1, 0), (0, -1), (0, 1), (-1, -1), (-1, 1), (1, -1), (1, 1))
-UNITS_AFTER = (2, 1, 1, 0)
-UNITS_BACK = (0, 1, 1, 0)
+EVENTS = (0, 1, 0, 1, 2, 0, 2, 1, 0, 2, 1, 0, 0, 2, 1, 1, 2, 0, 2, 1, 2, 0, 1, 2)
+DOUBLE = (1, 4)
 
 
 def shift_by_one(cells, axis):
@@ -92,37 +92,40 @@
                 offset = 9 * ox + 3 * oy + oz
                 terms_ref[offset * width : (offset + 1) * width] = term.T
 
-    def features_unit(tensor, ox, acc):
-        for oy in range(3):
-            first = 9 * ox + 3 * oy
-            if tensor == 0:
-                rhs = w_ref[first : first + 3].reshape(3 * width, width)
+    def features_unit(tensor, ox, oy, acc):
+        first = 9 * ox + 3 * oy
+        if tensor == 0:
+            rhs = w_ref[first : first + 3].reshape(3 * width, width)
+        else:
+            rhs = jnp.concatenate([w_ref[26 - first - oz] for oz in range(3)], 1)
+        for brick in range(slots):
+            rows = slice(512 * brick, 512 * brick + 512)
+            lhs = jnp.concatenate([window(tensor, brick, ox, oy, oz) for oz in range(3)], 1)
+            part = lax.dot_general(
+                lhs, rhs, (((1,), (tensor,)), ((), ())), preferred_element_type=jnp.float32
+            )
+            if first == 0:
+                acc[rows] = part
             else:
-                rhs = jnp.concatenate([w_ref[26 - first - oz] for oz in range(3)], 1)
-            for brick in range(slots):
-                rows = slice(512 * brick, 512 * brick + 512)
-                lhs = jnp.concatenate([window(tensor, brick, ox, oy, oz) for oz in range(3)], 1)
-                part = lax.dot_general(
-                    lhs, rhs, (((1,), (tensor,)), ((), ())), preferred_element_type=jnp.float32
-                )
-                if ox == 0 and oy == 0:
-                    acc[rows] = part
-                else:
-                    acc[rows] += part
-
-    def units(accs):
+                acc[rows] += part
+
+    def units(accs, prepare):
         for tensor, acc, target in ((0, accs[0], out_ref), (1, accs[1], back_ref)):
+            for action in prepare[tensor]:
+                action()
+                yield
             for ox in range(3):
-                features_unit(tensor, ox, acc)
-                if ox == 2:
-                    target[...] = acc[...].astype(target.dtype)
-                yield
+                for oy in range(3):
+                    features_unit(tensor, ox, oy, acc)
+                    if ox == 2 and oy == 2:
+                        target[...] = acc[...].astype(target.dtype)
+                    yield
 
     if plan is None:
         terms_ref, *accs = rest
         for ox in range(3):
             grad_terms(ox, terms_ref)
-        for _ in units(accs):
+        for _ in units(accs, ((), ())):
             pass
         return
 
@@ -214,16 +217,49 @@
     def rows_of(value):
         return value.reshape(-1, width).astype(jnp.bfloat16)
 
-    @pl.loop(0, 2 * slots)
-    def _(i):
-        tensor, brick = i // slots, i % slots
-
-        @pl.loop(0, 8)
-        def _(x):
-            sources = [cells(both_ref[tensor, slot, x]) for slot in range(slots)]
-            for oz, value in enumerate(extended_z(sources, brick, 12)):
-                odd_ref[oz, tensor, brick, x + 1] = rows_of(value)
-
+    def build_center(tensor):
+        @pl.loop(0, slots)
+        def _(brick):
+
+            @pl.loop(0, 8)
+            def _(x):
+                sources = [cells(both_ref[tensor, slot, x]) for slot in range(slots)]
+                for oz, value in enumerate(extended_z(sources, brick, 12)):
+                    odd_ref[oz, tensor, brick, x + 1] = rows_of(value)
+
+    def build_edges(tensor):
+        @pl.loop(0, slots)
+        def _(brick):
+            for end in range(2):
+                sources = [cells(halo_y[end, tensor, slot]) for slot in range(slots)]
+                for oz, value in enumerate(extended_z(sources, brick, 9 + 6 * end)):
+                    edge_y[oz, end] = value
+
+            @pl.loop(0, 8)
+            def _(x):
+                for oz in range(3):
+                    middle = cells(odd_ref[oz, tensor, brick, x + 1])
+                    row = jnp.concatenate([edge_y[oz, 0, pl.ds(x, 1)], middle, edge_y[oz, 1, pl.ds(x, 1)]], 0)
+                    even_ref[oz, tensor, brick, x + 1] = rows_of(row)
+
+            for end in range(2):
+                first = 18 * end
+                middle = extended_z(
+                    [cells(halo_x[end, tensor, slot]) for slot in range(slots)], brick, first + 3
+                )
+                ends = []
+                for end_y in range(2):
+                    column = [
+                        halo_corner[end, end_y, tensor, slot].astype(jnp.float32)[None, :8]
+                        for slot in range(slots)
+                    ]
+                    ends.append(extended_z(column, brick, first + 6 * end_y))
+                for oz in range(3):
+                    row = jnp.concatenate([ends[0][oz], middle[oz], ends[1][oz]], 0)
+                    even_ref[oz, tensor, brick, 9 * end] = rows_of(row)
+                    odd_ref[oz, tensor, brick, 9 * end] = rows_of(middle[oz])
+
+    build_center(0)
     for slot, step in enumerate(HALO):
         dst, arriving = halo_copy(slot, 1)
 
@@ -235,38 +271,7 @@
         def _():
             dst[...] = jnp.zeros(dst.shape, dst.dtype)
 
-    @pl.loop(0, 2 * slots)
-    def _(i):
-        tensor, brick = i // slots, i % slots
-        for end in range(2):
-            sources = [cells(halo_y[end, tensor, slot]) for slot in range(slots)]
-            for oz, value in enumerate(extended_z(sources, brick, 9 + 6 * end)):
-                edge_y[oz, end] = value
-
-        @pl.loop(0, 8)
-        def _(x):
-            for oz in range(3):
-                middle = cells(odd_ref[oz, tensor, brick, x + 1])
-                row = jnp.concatenate([edge_y[oz, 0, pl.ds(x, 1)], middle, edge_y[oz, 1, pl.ds(x, 1)]], 0)
-                even_ref[oz, tensor, brick, x + 1] = rows_of(row)
-
-        for end in range(2):
-            first = 18 * end
-            middle = extended_z(
-                [cells(halo_x[end, tensor, slot]) for slot in range(slots)], brick, first + 3
-            )
-            ends = []
-            for end_y in range(2):
-                column = [
-                    halo_corner[end, end_y, tensor, slot].astype(jnp.float32)[None, :8]
-                    for slot in range(slots)
-                ]
-                ends.append(extended_z(column, brick, first + 6 * end_y))
-            for oz in range(3):
-                row = jnp.concatenate([ends[0][oz], middle[oz], ends[1][oz]], 0)
-                even_ref[oz, tensor, brick, 9 * end] = rows_of(row)
-                odd_ref[oz, tensor, brick, 9 * end] = rows_of(middle[oz])
-
+    build_edges(0)
     side = bit_of(pair)
     mine = pl.ds(pl.multiple_of(side * LANES, LANES), LANES)
     other = pl.ds(pl.multiple_of((1 - side) * LANES, LANES), LANES)
@@ -295,7 +300,13 @@
     def rows_at(first):
         return pl.ds(pl.multiple_of(first, 16), block)
 
-    def send_coded(stage, part, bit):
+    def send_coded(stage, part, bit, blocks, source):
+        @pl.loop(0, blocks)
+        def _(i):
+            code, unit = encode(source(i))
+            code_to[stage][part, rows_at(i * block)] = code
+            unit_to[stage][part, i] = unit
+
         send(
             [
                 (code_to[stage].at[part], code_in[stage].at[part]),
@@ -306,75 +317,68 @@
             bit,
         )
 
-    work = units(accs)
-    base = [0] * PARTS
-    for p in range(PARTS):
-        grad_terms(p, terms_ref)
-
-        @pl.loop(0, part_blocks)
-        def _(i):
-            code, unit = encode(terms_ref[rows_at(p * part_rows + i * block), other])
-            code_to[0][p, rows_at(i * block)] = code
-            unit_to[0][p, i] = unit
-
-        send_coded(0, p, pair)
-
-    for stage in range(stages):
-        blocks = part_blocks >> stage
-        for p in range(PARTS):
+    def send_sum(step, part, bit, first, blocks):
+        rows = pl.ds(pl.multiple_of(part * part_rows + first * block, 16), blocks * block)
+        code_span = code_out.at[rows, mine]
+        unit_span = unit_out.at[side, pl.ds(part * part_blocks + first, blocks)]
+        send([(code_span, code_span), (unit_span, unit_span)], step, part, bit)
+
+    def travel(p):
+        start = p * part_rows
+        send_coded(0, p, pair, part_blocks, lambda i: terms_ref[rows_at(start + i * block), other])
+        yield
+        base = 0
+        for stage in range(stages):
+            blocks = part_blocks >> stage
             arrived(p)
 
             @pl.loop(0, blocks)
             def _(i):
                 value = decode(code_in[stage][p, rows_at(i * block)], unit_in[stage][p, i])
                 if stage == 0:
-                    own = terms_ref[rows_at(p * part_rows + i * block), mine]
+                    own = terms_ref[rows_at(start + i * block), mine]
                 else:
-                    own = acc[p, rows_at((base[p] + i) * block)]
-                acc[p, rows_at((base[p] + i) * block)] = own + value
+                    own = acc[p, rows_at((base + i) * block)]
+                acc[p, rows_at((base + i) * block)] = own + value
 
             if stage < stages - 1:
                 bit = orders[p][stage]
                 half = blocks // 2
-                away = base[p] + (1 - bit_of(bit)) * half
-                base[p] = base[p] + bit_of(bit) * half
-
-                @pl.loop(0, half)
-                def _(i):
-                    code, unit = encode(acc[p, rows_at((away + i) * block)])
-                    code_to[stage + 1][p, rows_at(i * block)] = code
-                    unit_to[stage + 1][p, i] = unit
-
-                send_coded(stage + 1, p, bit)
+                away = base + (1 - bit_of(bit)) * half
+                base = base + bit_of(bit) * half
+                send_coded(stage + 1, p, bit, half, lambda i: acc[p, rows_at((away + i) * block)])
             else:
-                code, unit = encode(acc[p, rows_at(base[p] * block)] * scale)
-                code_out[rows_at(p * part_rows + base[p] * block), mine] = code
-                unit_out[side, p * part_blocks + base[p]] = unit
-        for _ in range(UNITS_AFTER[stage] if stage < stages - 1 else 0):
+                code, unit = encode(acc[p, rows_at(base * block)] * scale)
+                code_out[rows_at(start + base * block), mine] = code
+                unit_out[side, p * part_blocks + base] = unit
+                send_sum(stages, p, orders[p][-1], base, 1)
+            yield
+        for level in range(stages - 2, -1, -1):
+            arrived(p)
+            blocks = part_blocks >> level
+            base = base - bit_of(orders[p][level]) * (blocks // 2)
+            bit = orders[p][level - 1] if level > 0 else pair
+            send_sum(2 * stages - 1 - level, p, bit, base, blocks)
+            yield
+        arrived(p)
+        yield
+
+    build_back = (lambda: build_center(1), lambda: build_edges(1))
+    work = units(accs, ((), build_back))
+    ways = [travel(p) for p in range(PARTS)]
+    for p in range(PARTS):
+        grad_terms(p, terms_ref)
+        next(ways[p])
+        if p > 0:
+            next(ways[p - 1])
+    next(ways[PARTS - 1])
+    for event, p in enumerate(EVENTS):
+        for _ in range(2 if event in DOUBLE else 1):
             next(work, None)
-        if stage < stages - 1:
-            continue
-        for p in range(PARTS):
-            code_span = code_out.at[rows_at(p * part_rows + base[p] * block), mine]
-            unit_span = unit_out.at[side, pl.ds(p * part_blocks + base[p], 1)]
-            send([(code_span, code_span), (unit_span, unit_span)], stages, p, orders[p][-1])
-
-    for back in range(1, stages + 1):
-        level = stages - 1 - back
-        for p in range(PARTS):
-            arrived(p)
-            if level < 0:
-                continue
-            blocks = part_blocks >> level
-            base[p] = base[p] - bit_of(orders[p][level]) * (blocks // 2)
-            first = pl.multiple_of(p * part_rows + base[p] * block, 16)
-            code_span = code_out.at[pl.ds(first, blocks * block), mine]
-            unit_span = unit_out.at[side, pl.ds(p * part_blocks + base[p], blocks)]
-            bit = orders[p][level - 1] if level > 0 else pair
-            send([(code_span, code_span), (unit_span, unit_span)], stages + back, p, bit)
-        if level >= 0:
-            for _ in range(UNITS_BACK[back - 1]):
-                next(work, None)
+        next(ways[p])
+    for way in ways:
+        for _ in way:
+            pass
     for _ in work:
         pass
     for copy in started:
@@ -390,7 +394,7 @@
     if sizes["gx"] != 8 or sizes["gy"] != 4 or rows % (PARTS * 16 * 16):
         return None
     pair, x, y, z_near, z_far = ("gy", 1), ("gy", 2), ("gx", 1), ("gx", 2), ("gx", 4)
-    return pair, [[x, y, z_near, z_far], [y, x, z_near, z_far], [z_near, z_far, x, y]]
+    return pair, [[z_near, z_far, x, y], [x, y, z_near, z_far], [y, x, z_near, z_far]]
 
 
 def conv(plan, slots, scale, *operands):
@@ -447,28 +451,39 @@
     )(*operands)
 
 
-def decode_kernel(code_ref, unit_ref, out_ref):
+def finish_kernel(code_ref, unit_ref, feature_ref, grad_ref, mask_ref, sum_ref, feature_out, grad_out):
+    for source, target in ((feature_ref, feature_out), (grad_ref, grad_out)):
+        target[...] = (source[...].astype(jnp.float32) * mask_ref[...]).astype(target.dtype)
     steps = unit_ref.shape[1]
     block = code_ref.shape[0] // steps
     for i in range(steps):
         for side in range(2):
             at = slice(i * block, (i + 1) * block), slice(side * LANES, (side + 1) * LANES)
-            out_ref[at] = decode(code_ref[at], unit_ref[side, i])
-
-
-def decode_all(code, unit):
+            sum_ref[at] = decode(code_ref[at], unit_ref[side, i])
+
+
+def finish(code, unit, out, back, mask):
     rows, width = code.shape
     steps = 8
     tile = pl.BlockSpec((rows // steps, width), lambda i: (i, 0))
+    voxels = pl.BlockSpec((out.shape[0] // steps, width), lambda i: (i, 0))
+    flags = pl.BlockSpec((out.shape[0] // steps, 1), lambda i: (i, 0))
+    units = pl.BlockSpec((2, unit.shape[1] // steps, 1, LANES), lambda i: (0, i, 0, 0))
     return pl.pallas_call(
-        decode_kernel,
+        finish_kernel,
         grid=(steps,),
-        in_specs=[tile, pl.BlockSpec((2, unit.shape[1] // steps, 1, LANES), lambda i: (0, i, 0, 0))],
-        out_specs=tile,
-        out_shape=jax.ShapeDtypeStruct(code.shape, jnp.float32),
+        in_specs=[tile, units, voxels, voxels, flags],
+        out_specs=[tile, voxels, voxels],
+        out_shape=[
+            jax.ShapeDtypeStruct(code.shape, jnp.float32),
+            jax.ShapeDtypeStruct(out.shape, out.dtype),
+            jax.ShapeDtypeStruct(back.shape, back.dtype),
+        ],
         compiler_params=pltpu.CompilerParams(vmem_limit_bytes=24 * 2**20),
-        cost_estimate=pl.CostEstimate(flops=2 * rows * width, bytes_accessed=6 * rows * width, transcendentals=0),
-    )(code, unit)
+        cost_estimate=pl.CostEstimate(
+            flops=2 * rows * width, bytes_accessed=8 * rows * width, transcendentals=0
+        ),
+    )(code, unit, out, back, mask)
 
 
 def shards(plan, features, cotangent, kernel, occupancy, neighbors):
@@ -496,11 +511,14 @@
     out, back, *total = conv(plan, slots, scale, *operands, kernel, grad_t)
     if plan is None:
         kernel_grad = lax.psum(total[0], ("gx", "gy")) * jnp.float32(scale)
+        flat_mask = mask_b.reshape(-1, 1)
+        out, back = out * flat_mask, back * flat_mask
     else:
-        kernel_grad = decode_all(*total)
+        mask = occupancy.reshape(-1, 1).astype(jnp.float32)
+        kernel_grad, out, back = finish(*total, out, back, mask)
     return (
-        out.reshape(features.shape) * mask_b,
-        back.reshape(features.shape) * mask_b,
+        out.reshape(features.shape),
+        back.reshape(features.shape),
         kernel_grad.reshape(kernel.shape),
     )
 

time: 91.9 us -> 98.2 us (1.069)
  Pallas kernels: 80.4 us -> 83.9 us
  local copies, waits for them, and re-layouts: 4.44 us -> 7.84 us
  other arithmetic: 6.14 us -> 4.67 us
    unnamed x6 -> x10, local copies, waits for them, and re-layouts: 1.7 us -> 5.1 us
    pallas_call x1, Pallas kernels: 76.1 us -> 79.4 us  [conv(): pl.pallas_call(functools.partial(conv_kernel, plan, slots, scale), in_spe...]
    mul x1 -> x0, other arithmetic: 1.55 us -> none  [shards(): back.reshape(features.shape) * mask_b]
where the time goes in v4:
time: 98.2 us; the launch traced here: 97.1 us
  Pallas kernels  83.9 us (85%)
  local copies, waits for them, and re-layouts  7.84 us (8%)
  other arithmetic  4.67 us (5%)
    pallas_call x1, Pallas kernels, conv(): pl.pallas_call(functools.partial(conv_kernel, plan, slots, scale), in_spe...  79.4 us
    unnamed x10, local copies, waits for them, and re-layouts  5.1 us
    pallas_call x1, Pallas kernels, finish(): pl.pallas_call(finish_kernel, grid=(steps,), in_specs=[tile, units, voxel...  4.43 us

profile of v4, /device:TPU:1, one launch (start us, length us, event | category | flops | bytes accessed | tf_op | source)
XLA Modules:
  0.0 97.1 jit_solution(6206989748784684446)
XLA Ops:
  0.6 0.8 broadcast_in_dim.8
  1.4 0.8 convert_bitcast_fusion
  2.2 0.1 convert_element_type.17
  2.3 0.7 broadcast_in_dim.9.refs_3_
  3.0 0.2 copy.27
  3.3 1.4 %copy_multiply_fusion.1 = (bf16[2,8,8,8,256]{4,3,0,1,2:T(8,128)(2,1)S(1)}, bf16[2,8,8,8,256]{4,3,0,1,2:T(8,128)(2,1)S(1)}) fusion(bf16[2,8,8,8,256]{4,3,2,1,0:T(8,128)(2,1)} %param.5, bf16[2,8,8,8]{3,0,1,2:T(2,128)(2,1)S(1)} %copy.14, bf16[2,8,8,8,256]{4,3,2,1,0:T(8,128)(2,1)} %param.6), kind=kLoop, calls=%fused_computation.3 | loop fusion | flops 524288 | bytes 2099200 | tf_op jit(solution)/shard_map/mul | solution.py:493
  4.7 0.7 fusion.2.refs_2_
  5.4 0.7 pad_maximum_fusion.1.refs_1_
  6.2 1.0 %copy.24 = bf16[1024,256]{0,1:T(8,128)(2,1)} copy(bf16[1024,256]{1,0:T(8,128)(2,1)S(1)} %bitcast.34) | data formatting | bytes 1048576 | tf_op jit(solution)/shard_map/reshape | solution.py:496
  7.3 1.1 %pad_maximum_fusion.refs_0_ = bf16[2,2,8,64,256]{4,3,2,1,0:T(8,128)(2,1)} fusion(bf16[1,2,8,64,256]{4,3,2,1,0:T(8,128)(2,1)S(1)} %bitcast.35, bf16[1,2,8,64,256]{4,3,2,1,0:T(8,128)(2,1)S(1)} %bitcast.36), kind=kLoop, calls=%fused_computation | loop fusion | flops 524288 | bytes 2097152 | tf_op jit(solution)/shard_map/stack | solution.py:495
  8.3 79.4 %shard_map.76 = (bf16[1024,256]{1,0:T(8,128)(2,1)}, bf16[1024,256]{1,0:T(8,128)(2,1)}, s16[6912,256]{1,0:T(8,128)(2,1)}, f32[2,48,1,128]{3,2,1,0:T(1,128)}) custom-call(bf16[2,2,8,64,256]{4,3,2,1,0:T(8,128)(2,1)} %pad_maximum_fusion.refs_0_, bf16[2,2,2,64,256]{4,3,2,1,0:T(8,128)(2,1)} %pad_maximum_fusion.1.refs_1_, ...), custom_call_target="tpu_custom_call" | custom-call | flops 10871635968 | bytes 25165824 | tf_op jit(solution)/shard_map/pallas_call | solution.py:441
  87.8 0.0 copy-start
  87.8 2.0 %copy-done = s16[6912,256]{1,0:T(8,128)(2,1)S(1)} copy-done((s16[6912,256]{1,0:T(8,128)(2,1)S(1)}, s16[6912,256]{1,0:T(8,128)(2,1)}, u32[]{:S(2)}) %copy-start) | copy-done | bytes 3538968
  89.8 0.0 copy-start.1
  89.8 1.0 %copy-done.1 = bf16[1024,256]{1,0:T(8,128)(2,1)S(1)} copy-done((bf16[1024,256]{1,0:T(8,128)(2,1)S(1)}, bf16[1024,256]{1,0:T(8,128)(2,1)}, u32[]{:S(2)}) %copy-start.1) | copy-done | bytes 524312
  90.8 0.0 copy-start.2
  90.8 1.0 %copy-done.2 = bf16[1024,256]{1,0:T(8,128)(2,1)S(1)} copy-done((bf16[1024,256]{1,0:T(8,128)(2,1)S(1)}, bf16[1024,256]{1,0:T(8,128)(2,1)}, u32[]{:S(2)}) %copy-start.2) | copy-done | bytes 524312
  91.9 0.0 copy-start.3
  91.9 0.8 copy-done.3
  92.7 4.4 %shard_map.77 = (f32[6912,256]{1,0:T(8,128)}, bf16[1024,256]{1,0:T(8,128)(2,1)}, bf16[1024,256]{1,0:T(8,128)(2,1)}) custom-call(s16[6912,256]{1,0:T(8,128)(2,1)S(1)} %copy-done, f32[2,48,1,128]{3,2,1,0:T(1,128)S(1)} %copy-done.3, bf16[1024,256]{1,0:T(8,128)(2,1)S(1)} %copy-done.1, bf16[1024,256]{1,0:T(8,128)(2,1)S(1)} %copy-done.2, f32[1024,1]{1,0:T(8,128)S(1)} %bitcast.31), custom_call_target="tpu_custom_call" | custom-call | flops 3538944 | bytes 14155776 | tf_op jit(solution)/shard_map/pallas_call | solution.py:472
  (7 shorter events, 0.2 us)
Async XLA Ops:
  87.8 2.0 %copy-start = (s16[6912,256]{1,0:T(8,128)(2,1)S(1)}, s16[6912,256]{1,0:T(8,128)(2,1)}, u32[]{:S(2)}) copy-start(s16[6912,256]{1,0:T(8,128)(2,1)} %get-tuple-element.10.code_ref) | copy-start | bytes 10616836
  89.8 1.0 %copy-start.1 = (bf16[1024,256]{1,0:T(8,128)(2,1)S(1)}, bf16[1024,256]{1,0:T(8,128)(2,1)}, u32[]{:S(2)}) copy-start(bf16[1024,256]{1,0:T(8,128)(2,1)} %get-tuple-element.12.feature_ref) | copy-start | bytes 1572868
  90.8 1.0 %copy-start.2 = (bf16[1024,256]{1,0:T(8,128)(2,1)S(1)}, bf16[1024,256]{1,0:T(8,128)(2,1)}, u32[]{:S(2)}) copy-start(bf16[1024,256]{1,0:T(8,128)(2,1)} %get-tuple-element.13.grad_ref) | copy-start | bytes 1572868
  91.9 0.8 copy-start.3

commit v5 on v3

--- a/solution.py
+++ b/solution.py
@@ -12,7 +12,7 @@
 PARTS = 3
 LANES = 128
 HALO = ((-1, 0), (1, 0), (0, -1), (0, 1), (-1, -1), (-1, 1), (1, -1), (1, 1))
-UNITS_AFTER = (2, 1, 1, 0)
+UNITS_AFTER = (2, 2, 1, 0)
 UNITS_BACK = (0, 1, 1, 0)
 
 
@@ -110,8 +110,11 @@
                 else:
                     acc[rows] += part
 
-    def units(accs):
+    def units(accs, prepare):
         for tensor, acc, target in ((0, accs[0], out_ref), (1, accs[1], back_ref)):
+            if tensor == 1:
+                prepare()
+                yield
             for ox in range(3):
                 features_unit(tensor, ox, acc)
                 if ox == 2:
@@ -122,7 +125,7 @@
         terms_ref, *accs = rest
         for ox in range(3):
             grad_terms(ox, terms_ref)
-        for _ in units(accs):
+        for _ in units(accs, lambda: None):
             pass
         return
 
@@ -214,16 +217,49 @@
     def rows_of(value):
         return value.reshape(-1, width).astype(jnp.bfloat16)
 
-    @pl.loop(0, 2 * slots)
-    def _(i):
-        tensor, brick = i // slots, i % slots
-
-        @pl.loop(0, 8)
-        def _(x):
-            sources = [cells(both_ref[tensor, slot, x]) for slot in range(slots)]
-            for oz, value in enumerate(extended_z(sources, brick, 12)):
-                odd_ref[oz, tensor, brick, x + 1] = rows_of(value)
-
+    def build_center(tensor):
+        @pl.loop(0, slots)
+        def _(brick):
+
+            @pl.loop(0, 8)
+            def _(x):
+                sources = [cells(both_ref[tensor, slot, x]) for slot in range(slots)]
+                for oz, value in enumerate(extended_z(sources, brick, 12)):
+                    odd_ref[oz, tensor, brick, x + 1] = rows_of(value)
+
+    def build_edges(tensor):
+        @pl.loop(0, slots)
+        def _(brick):
+            for end in range(2):
+                sources = [cells(halo_y[end, tensor, slot]) for slot in range(slots)]
+                for oz, value in enumerate(extended_z(sources, brick, 9 + 6 * end)):
+                    edge_y[oz, end] = value
+
+            @pl.loop(0, 8)
+            def _(x):
+                for oz in range(3):
+                    middle = cells(odd_ref[oz, tensor, brick, x + 1])
+                    row = jnp.concatenate([edge_y[oz, 0, pl.ds(x, 1)], middle, edge_y[oz, 1, pl.ds(x, 1)]], 0)
+                    even_ref[oz, tensor, brick, x + 1] = rows_of(row)
+
+            for end in range(2):
+                first = 18 * end
+                middle = extended_z(
+                    [cells(halo_x[end, tensor, slot]) for slot in range(slots)], brick, first + 3
+                )
+                ends = []
+                for end_y in range(2):
+                    column = [
+                        halo_corner[end, end_y, tensor, slot].astype(jnp.float32)[None, :8]
+                        for slot in range(slots)
+                    ]
+                    ends.append(extended_z(column, brick, first + 6 * end_y))
+                for oz in range(3):
+                    row = jnp.concatenate([ends[0][oz], middle[oz], ends[1][oz]], 0)
+                    even_ref[oz, tensor, brick, 9 * end] = rows_of(row)
+                    odd_ref[oz, tensor, brick, 9 * end] = rows_of(middle[oz])
+
+    build_center(0)
     for slot, step in enumerate(HALO):
         dst, arriving = halo_copy(slot, 1)
 
@@ -235,38 +271,7 @@
         def _():
             dst[...] = jnp.zeros(dst.shape, dst.dtype)
 
-    @pl.loop(0, 2 * slots)
-    def _(i):
-        tensor, brick = i // slots, i % slots
-        for end in range(2):
-            sources = [cells(halo_y[end, tensor, slot]) for slot in range(slots)]
-            for oz, value in enumerate(extended_z(sources, brick, 9 + 6 * end)):
-                edge_y[oz, end] = value
-
-        @pl.loop(0, 8)
-        def _(x):
-            for oz in range(3):
-                middle = cells(odd_ref[oz, tensor, brick, x + 1])
-                row = jnp.concatenate([edge_y[oz, 0, pl.ds(x, 1)], middle, edge_y[oz, 1, pl.ds(x, 1)]], 0)
-                even_ref[oz, tensor, brick, x + 1] = rows_of(row)
-
-        for end in range(2):
-            first = 18 * end
-            middle = extended_z(
-                [cells(halo_x[end, tensor, slot]) for slot in range(slots)], brick, first + 3
-            )
-            ends = []
-            for end_y in range(2):
-                column = [
-                    halo_corner[end, end_y, tensor, slot].astype(jnp.float32)[None, :8]
-                    for slot in range(slots)
-                ]
-                ends.append(extended_z(column, brick, first + 6 * end_y))
-            for oz in range(3):
-                row = jnp.concatenate([ends[0][oz], middle[oz], ends[1][oz]], 0)
-                even_ref[oz, tensor, brick, 9 * end] = rows_of(row)
-                odd_ref[oz, tensor, brick, 9 * end] = rows_of(middle[oz])
-
+    build_edges(0)
     side = bit_of(pair)
     mine = pl.ds(pl.multiple_of(side * LANES, LANES), LANES)
     other = pl.ds(pl.multiple_of((1 - side) * LANES, LANES), LANES)
@@ -306,7 +311,11 @@
             bit,
         )
 
-    work = units(accs)
+    def build_back():
+        build_center(1)
+        build_edges(1)
+
+    work = units(accs, build_back)
     base = [0] * PARTS
     for p in range(PARTS):
         grad_terms(p, terms_ref)
@@ -447,28 +456,39 @@
     )(*operands)
 
 
-def decode_kernel(code_ref, unit_ref, out_ref):
+def finish_kernel(code_ref, unit_ref, feature_ref, grad_ref, mask_ref, sum_ref, feature_out, grad_out):
+    for source, target in ((feature_ref, feature_out), (grad_ref, grad_out)):
+        target[...] = (source[...].astype(jnp.float32) * mask_ref[...]).astype(target.dtype)
     steps = unit_ref.shape[1]
     block = code_ref.shape[0] // steps
     for i in range(steps):
         for side in range(2):
             at = slice(i * block, (i + 1) * block), slice(side * LANES, (side + 1) * LANES)
-            out_ref[at] = decode(code_ref[at], unit_ref[side, i])
-
-
-def decode_all(code, unit):
+            sum_ref[at] = decode(code_ref[at], unit_ref[side, i])
+
+
+def finish(code, unit, out, back, mask):
     rows, width = code.shape
     steps = 8
     tile = pl.BlockSpec((rows // steps, width), lambda i: (i, 0))
+    voxels = pl.BlockSpec((out.shape[0] // steps, width), lambda i: (i, 0))
+    flags = pl.BlockSpec((out.shape[0] // steps, 1), lambda i: (i, 0))
+    units = pl.BlockSpec((2, unit.shape[1] // steps, 1, LANES), lambda i: (0, i, 0, 0))
     return pl.pallas_call(
-        decode_kernel,
+        finish_kernel,
         grid=(steps,),
-        in_specs=[tile, pl.BlockSpec((2, unit.shape[1] // steps, 1, LANES), lambda i: (0, i, 0, 0))],
-        out_specs=tile,
-        out_shape=jax.ShapeDtypeStruct(code.shape, jnp.float32),
-        compiler_params=pltpu.CompilerParams(vmem_limit_bytes=24 * 2**20),
-        cost_estimate=pl.CostEstimate(flops=2 * rows * width, bytes_accessed=6 * rows * width, transcendentals=0),
-    )(code, unit)
+        in_specs=[tile, units, voxels, voxels, flags],
+        out_specs=[tile, voxels, voxels],
+        out_shape=[
+            jax.ShapeDtypeStruct(code.shape, jnp.float32),
+            jax.ShapeDtypeStruct(out.shape, out.dtype),
+            jax.ShapeDtypeStruct(back.shape, back.dtype),
+        ],
+        compiler_params=pltpu.CompilerParams(vmem_limit_bytes=58 * 2**20),
+        cost_estimate=pl.CostEstimate(
+            flops=2 * rows * width, bytes_accessed=8 * rows * width, transcendentals=0
+        ),
+    )(code, unit, out, back, mask)
 
 
 def shards(plan, features, cotangent, kernel, occupancy, neighbors):
@@ -496,11 +516,14 @@
     out, back, *total = conv(plan, slots, scale, *operands, kernel, grad_t)
     if plan is None:
         kernel_grad = lax.psum(total[0], ("gx", "gy")) * jnp.float32(scale)
+        flat_mask = mask_b.reshape(-1, 1)
+        out, back = out * flat_mask, back * flat_mask
     else:
-        kernel_grad = decode_all(*total)
+        mask = occupancy.reshape(-1, 1).astype(jnp.float32)
+        kernel_grad, out, back = finish(*total, out, back, mask)
     return (
-        out.reshape(features.shape) * mask_b,
-        back.reshape(features.shape) * mask_b,
+        out.reshape(features.shape),
+        back.reshape(features.shape),
         kernel_grad.reshape(kernel.shape),
     )
 

time: 91.9 us -> 92.9 us (1.011)
  Pallas kernels: 80.4 us -> 83.4 us
  other arithmetic: 6.14 us -> 4.67 us
    pallas_call x1, Pallas kernels: 4.29 us -> 7.72 us  [finish(): pl.pallas_call(finish_kernel, grid=(steps,), in_specs=[tile, units, voxel...]
    mul x1 -> x0, other arithmetic: 1.55 us -> none  [shards(): back.reshape(features.shape) * mask_b]
where the time goes in v5:
time: 92.9 us; the launch traced here: 92.6 us
  Pallas kernels  83.4 us (90%)
  other arithmetic  4.67 us (5%)
  local copies, waits for them, and re-layouts  3.8 us (4%)
    pallas_call x1, Pallas kernels, conv(): pl.pallas_call(functools.partial(conv_kernel, plan, slots, scale), in_spe...  75.7 us
    pallas_call x1, Pallas kernels, finish(): pl.pallas_call(finish_kernel, grid=(steps,), in_specs=[tile, units, voxel...  7.72 us

profile of v5, /device:TPU:1, one launch (start us, length us, event | category | flops | bytes accessed | tf_op | source)
XLA Modules:
  0.0 92.6 jit_solution(10490708435313360258)
XLA Ops:
  0.6 0.8 broadcast_in_dim.8
  1.4 0.8 convert_bitcast_fusion
  2.2 0.1 convert_element_type.17
  2.3 0.7 broadcast_in_dim.9.refs_3_
  3.1 1.0 %copy.27 = f32[1,1024]{0,1:T(8,128)} copy(f32[1,1024]{1,0:T(1,128)S(1)} %bitcast.40) | data formatting | bytes 8192
  4.1 1.4 %copy_multiply_fusion.1 = (bf16[2,8,8,8,256]{4,3,0,1,2:T(8,128)(2,1)S(1)}, bf16[2,8,8,8,256]{4,3,0,1,2:T(8,128)(2,1)S(1)}) fusion(bf16[2,8,8,8,256]{4,3,2,1,0:T(8,128)(2,1)} %param.5, bf16[2,8,8,8]{3,0,1,2:T(2,128)(2,1)S(1)} %copy.14, bf16[2,8,8,8,256]{4,3,2,1,0:T(8,128)(2,1)} %param.6), kind=kLoop, calls=%fused_computation.3 | loop fusion | flops 524288 | bytes 2099200 | tf_op jit(solution)/shard_map/mul | solution.py:498
  5.6 0.7 fusion.2.refs_2_
  6.3 0.7 pad_maximum_fusion.1.refs_1_
  7.0 1.0 %copy.24 = bf16[1024,256]{0,1:T(8,128)(2,1)} copy(bf16[1024,256]{1,0:T(8,128)(2,1)S(1)} %bitcast.33) | data formatting | bytes 1048576 | tf_op jit(solution)/shard_map/reshape | solution.py:501
  8.1 1.1 %pad_maximum_fusion.refs_0_ = bf16[2,2,8,64,256]{4,3,2,1,0:T(8,128)(2,1)} fusion(bf16[1,2,8,64,256]{4,3,2,1,0:T(8,128)(2,1)S(1)} %bitcast.34, bf16[1,2,8,64,256]{4,3,2,1,0:T(8,128)(2,1)S(1)} %bitcast.36), kind=kLoop, calls=%fused_computation | loop fusion | flops 524288 | bytes 2097152 | tf_op jit(solution)/shard_map/stack | solution.py:500
  9.2 75.7 %shard_map.76 = (bf16[1024,256]{1,0:T(8,128)(2,1)}, bf16[1024,256]{1,0:T(8,128)(2,1)}, s16[6912,256]{1,0:T(8,128)(2,1)}, f32[2,48,1,128]{3,2,1,0:T(1,128)}) custom-call(bf16[2,2,8,64,256]{4,3,2,1,0:T(8,128)(2,1)} %pad_maximum_fusion.refs_0_, bf16[2,2,2,64,256]{4,3,2,1,0:T(8,128)(2,1)} %pad_maximum_fusion.1.refs_1_, ...), custom_call_target="tpu_custom_call" | custom-call | flops 10871635968 | bytes 25165824 | tf_op jit(solution)/shard_map/pallas_call | solution.py:446
  84.9 7.7 %shard_map.77 = (f32[6912,256]{1,0:T(8,128)}, bf16[1024,256]{1,0:T(8,128)(2,1)}, bf16[1024,256]{1,0:T(8,128)(2,1)}) custom-call(s16[6912,256]{1,0:T(8,128)(2,1)} %get-tuple-element.10.code_ref, f32[2,48,1,128]{3,2,1,0:T(1,128)} %get-tuple-element.11.unit_ref, bf16[1024,256]{1,0:T(8,128)(2,1)} %get-tuple-element.12.feature_ref, ...), custom_call_target="tpu_custom_call" | custom-call | flops 3538944 | bytes 14155776 | tf_op jit(solution)/shard_map/pallas_call | solution.py:477
  (7 shorter events, 0.2 us)
